TPU v7x, 32 devices: a whole 2x2x4 slice. The times are simulated.
32 devices in a mesh: ctx: 16 (over z, y, x), fsdp: 2 (over core).
Axes of the slice: x: 2, y: 2, z: 4, core: 2. Of those that a mesh axis runs over, the one named last changes fastest.
Arguments:
- out_grad: bfloat16 [4096, 16384], P('fsdp', 'ctx'), may hold values from -6 to 6
- gate_values: bfloat16 [4096, 16384], P('fsdp', 'ctx'), may hold values from -6 to 6
- kv_product: bfloat16 [4096, 16384], P('fsdp', 'ctx'), may hold values from -6 to 6
- w_out: bfloat16 [4096, 4096], P('ctx', 'fsdp'), may hold values from -0.09375 to 0.09375
- filters: bfloat16 [2, 16, 128, 128], P('fsdp', 'ctx'), may hold values from -0.5 to 0.5
Outputs:
- gate_grad: float32 [4096, 16384], P('fsdp', 'ctx')
- kv_grad: bfloat16 [4096, 16384], P('fsdp', 'ctx')
- filter_grad: float32 [2, 16, 128, 128], P('fsdp', 'ctx')
- w_grad: float32 [4096, 4096], P('ctx', 'fsdp')
All inputs are finite; a program needn't handle non-finite values.
Results may differ from a plain program's by a relative error of at most 0.0049.
Values may be sent and summed in bfloat16 or wider, within the bound.
No kernel may reach another device: no remote copies, remote signals or barrier semaphores. Data moves between devices by JAX's collectives and lax.ppermute only.
A program may use at most 192 MiB of HBM per device.

v0:
```python
import math

import jax
import jax.numpy as jnp
from jax import lax
from jax.sharding import PartitionSpec as P


def toeplitz_pair(filters):
    channels, tap_count = filters.shape
    zero_pad = jnp.zeros_like(filters)

    def make_band(vector):
        tiled = jnp.tile(vector, (1, tap_count + 1))
        window_cut = tiled[:, tap_count : tap_count + tap_count * (2 * tap_count - 1)]
        return window_cut.reshape(channels, tap_count, 2 * tap_count - 1)[:, :, :tap_count]

    near_band = make_band(jnp.concatenate([zero_pad, filters], axis=1))
    far_band = make_band(jnp.concatenate([filters, zero_pad], axis=1))
    return (near_band, far_band)


def mixer_piece(filters, signal, signal_prior, cotangent, cotangent_after):
    channels, seq_len = signal.shape
    tap_count = filters.shape[1]
    blocks_count = seq_len // tap_count
    near_band, far_band = toeplitz_pair(filters)
    current = signal.reshape(channels, blocks_count, tap_count)
    previous = jnp.concatenate([signal_prior[:, None, :], current[:, :-1]], axis=1)
    grad_current = cotangent.reshape(channels, blocks_count, tap_count)
    grad_later = jnp.concatenate([grad_current[:, 1:], cotangent_after[:, None, :]], axis=1)
    wide = jnp.float32
    mixed = jnp.einsum("cbs,csr->cbr", current, near_band, preferred_element_type=wide)
    mixed = mixed + jnp.einsum("cbs,csr->cbr", previous, far_band, preferred_element_type=wide)
    signal_grad = jnp.einsum("cbr,csr->cbs", grad_current, near_band, preferred_element_type=wide)
    signal_grad = signal_grad + jnp.einsum(
        "cbr,csr->cbs", grad_later, far_band, preferred_element_type=wide
    )
    near_weight = jnp.einsum("cbs,cbr->csr", current, grad_current, preferred_element_type=wide)
    far_weight = jnp.einsum("cbs,cbr->csr", previous, grad_current, preferred_element_type=wide)
    band_pair, pullback = jax.vjp(toeplitz_pair, filters.astype(jnp.float32))
    filter_part = pullback((near_weight, far_weight))[0]
    return (mixed.reshape(channels, seq_len), signal_grad.reshape(channels, seq_len), filter_part)


def on_device(out_grad, gate_values, kv_product, w_out, filters):
    ctx_count = lax.axis_size("ctx")
    chan_count = filters.shape[2]
    tap_count = filters.shape[3]
    norm_scale = 1.0 / math.sqrt(ctx_count * out_grad.shape[1])
    grad_full = lax.all_gather(out_grad, "fsdp", axis=0, tiled=True)
    grad_part = grad_full
    mix_grad = lax.dot_general(
        lax.all_gather(w_out, "ctx", axis=0, tiled=True),
        grad_part,
        (((0,), (0,)), ((), ())),
        preferred_element_type=jnp.float32,
    )
    conv_grad = (mix_grad * gate_values.astype(jnp.float32)).astype(jnp.bfloat16)
    signal_chan, grad_chan = (
        lax.all_to_all(kv_product, "ctx", split_axis=0, concat_axis=1, tiled=True),
        lax.all_to_all(conv_grad, "ctx", split_axis=0, concat_axis=1, tiled=True),
    )
    own_filters = filters.reshape(chan_count, tap_count)
    edge_zero = jnp.zeros((chan_count, tap_count), jnp.bfloat16)
    mixed, signal_grad, filter_part = mixer_piece(
        own_filters, signal_chan, edge_zero, grad_chan, edge_zero
    )
    mixed_tok, kv_grad = (
        lax.all_to_all(mixed.astype(jnp.bfloat16), "ctx", split_axis=1, concat_axis=0, tiled=True),
        lax.all_to_all(
            signal_grad.astype(jnp.bfloat16), "ctx", split_axis=1, concat_axis=0, tiled=True
        ),
    )
    filter_grad = (filter_part * norm_scale).reshape(filters.shape)
    mixed_wide = mixed_tok.astype(jnp.float32)
    gate_grad = mix_grad * mixed_wide
    gated_rows = (gate_values.astype(jnp.float32) * mixed_wide).astype(jnp.bfloat16)
    grad_part = grad_full
    w_grad = (
        lax.psum_scatter(
            lax.dot_general(
                grad_part, gated_rows, (((1,), (1,)), ((), ())), preferred_element_type=jnp.float32
            ),
            "ctx",
            scatter_dimension=0,
            tiled=True,
        )
        * norm_scale
    )
    return (gate_grad, kv_grad, filter_grad, w_grad)


def solution(mesh):
    in_specs = (
        P("fsdp", "ctx"),
        P("fsdp", "ctx"),
        P("fsdp", "ctx"),
        P("ctx", "fsdp"),
        P("fsdp", "ctx", None, None),
    )
    out_specs = (P("fsdp", "ctx"), P("fsdp", "ctx"), P("fsdp", "ctx", None, None), P("ctx", "fsdp"))
    return jax.shard_map(
        on_device, mesh=mesh, in_specs=in_specs, out_specs=out_specs, check_vma=False
    )
```

profile of v0, /device:TPU:0, one launch (start us, length us, event | category | flops | bytes accessed | tf_op | source)
XLA Modules:
  0.0 1219.7 jit_solution(15633212577947132489)
XLA Ops:
  8.7 8.4 all-to-all-start
  23.8 9.9 reshape.81
  38.6 7.3 copy.61
  51.6 9.8 reshape.82
  66.1 6.7 copy.62
  72.8 46.5 %all-to-all-done = bf16[16,128,1024]{2,1,0:T(8,128)(2,1)} async-done(((bf16[16,128,1024]{2,1,0:T(8,128)(2,1)}), bf16[16,128,1024]{2,1,0:T(8,128)(2,1)}, u32[]{:S(2)}, u32[]{:S(2)}) %all-to-all-start) | async-done | bytes 4194336 | tf_op jit(solution)/shard_map/all_to_all | solution.py:61
  125.8 7.3 reshape.72
  133.2 10.1 fusion.7
  143.3 8.4 fusion.2
  151.7 7.2 copy.42
  158.9 209.7 %all_to_all.58 = bf16[128,16,1024]{0,2,1:T(8,128)(2,1)S(1)} all-to-all(bf16[128,16,1024]{0,2,1:T(8,128)(2,1)} %bitcast.52), channel_id=1, replica_groups=mesh['ctx'=16,'fsdp'=2] {'ctx'}, dimensions={1} | all-to-all | bytes 8388608 | tf_op jit(solution)/shard_map/all_to_all | solution.py:70
  372.9 9.2 copy.43
  382.1 26.1 %fusion.1 = (bf16[2048,1024]{1,0:T(8,128)(2,1)S(1)}, f32[2048,1024]{1,0:T(8,128)}, bf16[2048,1024]{1,0:T(8,128)(2,1)}) fusion(bf16[2048,1024]{1,0:T(8,128)(2,1)} %param.6, f32[16,128,1024]{2,1,0:T(8,128)} %copy.43, bf16[4096,2048]{1,0:T(8,128)(2,1)} %all-gather.3.cloned.1.call-done, bf16[4096,1024]{1,0:T(8,128)(2,1)} %all-gather.5.cloned.1.call-done), kind=kOutput, calls=%fused_computation.4 | convolution fusion | flops 17192452096 | bytes 54525952 | tf_op jit(solution)/shard_map/dot_general | solution.py:53
  408.2 21.5 %convolution_bitcast_fusion = f32[4096,2048]{0,1:T(8,128)} fusion(bf16[2048,1024]{1,0:T(8,128)(2,1)S(1)} %get-tuple-element.16, bf16[4096,1024]{1,0:T(8,128)(2,1)S(1)} %copy-done.6), kind=kOutput, calls=%fused_computation | convolution fusion | flops 17179869184 | bytes 46137344 | tf_op jit(solution)/shard_map/dot_general | solution.py:82
  429.7 141.7 %all_to_all.59 = bf16[16,128,1024]{2,1,0:T(8,128)(2,1)S(1)} all-to-all(bf16[16,128,1024]{2,1,0:T(8,128)(2,1)} %bitcast.55), channel_id=1, replica_groups=mesh['ctx'=16,'fsdp'=2] {'ctx'}, dimensions={0} | all-to-all | bytes 8388608 | tf_op jit(solution)/shard_map/all_to_all | solution.py:62
  575.7 7.3 reshape.74
  583.0 7.2 slice.29
  599.2 7.4 convert_element_type.41
  613.2 9.5 all-to-all-start.3
  622.7 8.3 convolution_bitcast_fusion.1
  631.0 9.0 copy.66
  640.1 11.2 pad.18.clone
  651.2 17.3 %reshape.77 = f32[128,32640]{1,0:T(8,128)} reshape(f32[128,128,255]{2,1,0:T(8,128)} %pad.18.clone) | data formatting | bytes 33423360 | tf_op jit(solution)/shard_map/transpose(jvp())/reshape | solution.py:16
  668.6 17.3 %copy.67 = f32[128,32640]{0,1:T(8,128)} copy(f32[128,32640]{1,0:T(8,128)} %reshape.77) | data formatting | bytes 33423360
  685.9 13.5 %pad.19.clone = f32[128,33024]{0,1:T(8,128)} pad(f32[128,32640]{0,1:T(8,128)} %copy.67, f32[]{:T(128)} %constant.4.clone.1), padding=0_0x128_256 | pad | bytes 33619972 | tf_op jit(solution)/shard_map/transpose(jvp())/pad | solution.py:15
  706.0 8.3 fusion.5
  714.3 11.1 pad.16
  725.4 17.4 %reshape.75 = f32[128,32640]{1,0:T(8,128)} reshape(f32[128,128,255]{2,1,0:T(8,128)} %pad.16) | data formatting | bytes 33423360 | tf_op jit(solution)/shard_map/transpose(jvp())/reshape | solution.py:16
  742.7 17.4 %copy.65 = f32[128,32640]{0,1:T(8,128)} copy(f32[128,32640]{1,0:T(8,128)} %reshape.75) | data formatting | bytes 33423360
  760.1 13.4 %pad.17.clone = f32[128,33024]{0,1:T(8,128)} pad(f32[128,32640]{0,1:T(8,128)} %copy.65, f32[]{:T(128)} %constant.4.clone.1), padding=0_0x128_256 | pad | bytes 33619972 | tf_op jit(solution)/shard_map/transpose(jvp())/pad | solution.py:15
  773.5 6.6 reduce_sum.18
  780.9 423.9 %reduce-scatter.2.cloned.1.call-done = f32[256,2048]{0,1:T(8,128)} async-done(((f32[4096,2048]{0,1:T(8,128)}), f32[256,2048]{0,1:T(8,128)}) %reduce-scatter.2.cloned.1.call-update) | async-done | bytes 2097168 | tf_op jit(solution)/shard_map/reduce_scatter | solution.py:81
  (43 shorter events, 69.8 us)
Async XLA Ops:
  7.2 374.9 %all-gather.5.cloned.1.call-start = ((), (), s32[]{:S(2)}) async-start(), calls=%async_computation.6 | async-start | bytes 12582912 | tf_op jit(solution)/shard_map/all_gather | solution.py:51
  7.9 374.2 %all-gather.3.cloned.1.call-start = ((), (), s32[]{:S(2)}) async-start(), calls=%async_computation.5 | async-start | bytes 17825792 | tf_op jit(solution)/shard_map/all_gather | solution.py:54
  8.6 8.4 copy-start.5
  8.7 110.7 %all-to-all-start = ((bf16[16,128,1024]{2,1,0:T(8,128)(2,1)}), bf16[16,128,1024]{2,1,0:T(8,128)(2,1)}, u32[]{:S(2)}, u32[]{:S(2)}) async-start(bf16[16,128,1024]{2,1,0:T(8,128)(2,1)} %bitcast.54), calls=%async_computation | async-start | bytes 8388608 | tf_op jit(solution)/shard_map/all_to_all | solution.py:61
  17.0 1187.8 %reduce-scatter.2.cloned.1.call-start = ((), (), s32[]{:S(2)}) async-start(), calls=%async_computation.7 | async-start | bytes 35651584 | tf_op jit(solution)/shard_map/reduce_scatter | solution.py:81
  133.2 10.1 copy-start.1
  133.2 10.1 copy-start.2
  382.1 26.1 %copy-start.6 = (bf16[4096,1024]{1,0:T(8,128)(2,1)S(1)}, bf16[4096,1024]{1,0:T(8,128)(2,1)}, u32[]{:S(2)}) copy-start(bf16[4096,1024]{1,0:T(8,128)(2,1)} %all-gather.5.cloned.1.call-done) | copy-start | bytes 25165828
  583.0 7.2 copy-start.4
  590.2 5.5 copy-start
  590.2 5.5 copy-start.3
  613.2 167.7 %all-to-all-start.3 = ((bf16[128,16,1024]{2,0,1:T(8,128)(2,1)}), bf16[128,16,1024]{2,0,1:T(8,128)(2,1)}, u32[]{:S(2)}, u32[]{:S(2)}) async-start(bf16[128,16,1024]{2,0,1:T(8,128)(2,1)} %copy.46), calls=%async_computation.3 | async-start | bytes 8388608 | tf_op jit(solution)/shard_map/all_to_all | solution.py:71
Sparse Core Ops, SparseCore 0:
  9.5 22.5 all-gather.4
  34.9 320.0 all-gather.2
  429.8 774.9 reduce-scatter.1
where the time goes:
time: 1240 us; the launch traced here: 1220 us
  waiting for transfers between devices  472 us (38%)
  blocking collectives  351 us (28%)
  local copies, waits for them, and re-layouts  254 us (20%)
  matrix products  91.7 us (7%)
  other arithmetic  19.2 us (2%)
  starting transfers between devices  18 us (1%)
  between operations  14 us (1%)
    reduce_scatter x1, waiting for transfers between devices, on_device(): lax.psum_scatter(lax.dot_general(grad_part, gated_rows, (((1,), (1,)), ((...  424 us
    all_to_all x1, blocking collectives, on_device(): lax.all_to_all(mixed.astype(jnp.bfloat16), 'ctx', split_axis=1, concat_ax...  210 us
    all_to_all x1, blocking collectives, on_device(): lax.all_to_all(conv_grad, 'ctx', split_axis=0, concat_axis=1, tiled=True)  142 us
    unnamed x23, local copies, waits for them, and re-layouts  65 us
    reshape x4, local copies, waits for them, and re-layouts, make_band(): window_cut.reshape(channels, tap_count, 2 * tap_count - 1)[:, :, :tap_count]  54.4 us
    all_to_all x1, waiting for transfers between devices, on_device(): lax.all_to_all(kv_product, 'ctx', split_axis=0, concat_axis=1, tiled=True)  46.5 us
    pad x2, local copies, waits for them, and re-layouts, make_band(): window_cut = tiled[:, tap_count:tap_count + tap_count * (2 * tap_count - 1)]  26.9 us
    dot_general x1, matrix products, on_device(): lax.dot_general(lax.all_gather(w_out, 'ctx', axis=0, tiled=True), grad_pa...  26.1 us
  transfers between devices with their start and end apart: 5, of which 2 were waited for; matrix products, arithmetic and copies ran while one was open for 25% of the time, Pallas kernels for 0%

commit v1 on v0

v1 whole, which is shorter than its diff:
```python
import functools
import math

import jax
import jax.numpy as jnp
from jax import lax
from jax.experimental import pallas as pl
from jax.experimental.pallas import tpu as pltpu
from jax.sharding import PartitionSpec as P

F32 = jnp.float32
BF16 = jnp.bfloat16
GROUP = 128
UNROLL = 8


def band_masks(taps):
    row = lax.broadcasted_iota(jnp.int32, (taps, taps), 0)
    lane = lax.broadcasted_iota(jnp.int32, (taps, taps), 1)
    return row, lane


def circulant(taps_row, taps):
    wide = jnp.broadcast_to(taps_row, (taps, taps))
    return pltpu.roll(wide, 0, 1, stride=1, stride_axis=0)


def mix_kernel(filt_ref, kv_ref, prior_ref, gate_ref, mixed_ref, gated_ref, cur, prev, out, filt):
    group, seq_len = kv_ref.shape
    taps = filt_ref.shape[1]
    blocks = seq_len // taps
    filt[...] = filt_ref[...].astype(F32)
    prev[:, 0, :] = prior_ref[...].astype(F32)
    for b in range(blocks):
        piece = kv_ref[:, b * taps : (b + 1) * taps].astype(F32)
        cur[:, b, :] = piece
        if b + 1 < blocks:
            prev[:, b + 1, :] = piece
    row, lane = band_masks(taps)
    near_mask = jnp.where(lane >= row, 1.0, 0.0).astype(BF16)

    def step(i, _):
        for u in range(UNROLL):
            c = i * UNROLL + u
            band = circulant(filt[pl.ds(c, 1), :], taps).astype(BF16)
            near = band * near_mask
            pair = jnp.concatenate([near, band - near], axis=0)
            data = jnp.concatenate([cur[c], prev[c]], axis=1).astype(BF16)
            out[c] = jnp.dot(data, pair, preferred_element_type=F32)
        return 0

    lax.fori_loop(0, group // UNROLL, step, 0)
    for b in range(blocks):
        span = slice(b * taps, (b + 1) * taps)
        mixed = out[:, b, :].astype(BF16)
        mixed_ref[:, span] = mixed
        gated_ref[:, span] = (gate_ref[:, span].astype(F32) * mixed.astype(F32)).astype(BF16)


def run_mix(filters, kv, prior, gate):
    chan, seq_len = kv.shape
    taps = filters.shape[1]
    blocks = seq_len // taps
    rows = lambda width: pl.BlockSpec((GROUP, width), lambda g: (g, 0))
    return pl.pallas_call(
        mix_kernel,
        grid=(chan // GROUP,),
        in_specs=[rows(taps), rows(seq_len), rows(taps), rows(seq_len)],
        out_specs=[rows(seq_len), rows(seq_len)],
        out_shape=[jax.ShapeDtypeStruct((chan, seq_len), BF16)] * 2,
        scratch_shapes=[pltpu.VMEM((GROUP, blocks, taps), F32)] * 3 + [pltpu.VMEM((GROUP, taps), F32)],
        compiler_params=pltpu.CompilerParams(vmem_limit_bytes=32 * 1024 * 1024),
        name="mix_kernel",
    )(filters, kv, prior, gate)


def grad_kernel(
    back_ref, grad_ref, after_ref, kv_ref, kv_grad_ref, filt_ref, cur, later, sig, out, back, total
):
    group, seq_len = kv_ref.shape
    taps = back_ref.shape[1]
    blocks = seq_len // taps
    back[...] = back_ref[...].astype(F32)
    later[:, blocks - 1, :] = after_ref[...].astype(F32)
    row, lane = band_masks(taps)
    flip = jnp.where(row + lane == taps - 1, 1.0, 0.0).astype(BF16)
    for b in range(blocks):
        span = slice(b * taps, (b + 1) * taps)
        piece = grad_ref[:, span].astype(F32)
        cur[:, b, :] = piece
        if b > 0:
            later[:, b - 1, :] = piece
        sig[:, b, :] = jnp.dot(kv_ref[:, span], flip, preferred_element_type=F32)
    near_mask = jnp.where(row >= lane, 1.0, 0.0).astype(BF16)
    upper = lane + row >= taps - 1

    def step(i, _):
        for u in range(UNROLL):
            c = i * UNROLL + u
            band = circulant(back[pl.ds(c, 1), :], taps).astype(BF16)
            near = band * near_mask
            pair = jnp.concatenate([near, band - near], axis=0)
            data = jnp.concatenate([cur[c], later[c]], axis=1).astype(BF16)
            out[c] = jnp.dot(data, pair, preferred_element_type=F32)
            outer = lax.dot_general(
                sig[c].astype(BF16), data, (((0,), (0,)), ((), ())), preferred_element_type=F32
            )
            joint = jnp.where(upper, outer[:, :taps], outer[:, taps:])
            skew = pltpu.roll(joint, 1, 1, stride=1, stride_axis=0)
            total[pl.ds(c, 1), :] = jnp.sum(skew, axis=0, keepdims=True)
        return 0

    lax.fori_loop(0, group // UNROLL, step, 0)
    for b in range(blocks):
        kv_grad_ref[:, b * taps : (b + 1) * taps] = out[:, b, :].astype(BF16)
    filt_ref[...] = total[...]


def run_grad(back, grad, after, kv):
    chan, seq_len = kv.shape
    taps = back.shape[1]
    blocks = seq_len // taps
    rows = lambda width: pl.BlockSpec((GROUP, width), lambda g: (g, 0))
    return pl.pallas_call(
        grad_kernel,
        grid=(chan // GROUP,),
        in_specs=[rows(taps), rows(seq_len), rows(taps), rows(seq_len)],
        out_specs=[rows(seq_len), rows(taps)],
        out_shape=[
            jax.ShapeDtypeStruct((chan, seq_len), BF16),
            jax.ShapeDtypeStruct((chan, taps), F32),
        ],
        scratch_shapes=[pltpu.VMEM((GROUP, blocks, taps), F32)] * 4
        + [pltpu.VMEM((GROUP, taps), F32)] * 2,
        compiler_params=pltpu.CompilerParams(vmem_limit_bytes=32 * 1024 * 1024),
        name="grad_kernel",
    )(back, grad, after, kv)


def on_device(out_grad, gate_values, kv_product, w_out, filters):
    ctx_count = lax.axis_size("ctx")
    chan_count = filters.shape[2]
    taps = filters.shape[3]
    seq_len = out_grad.shape[1]
    norm_scale = 1.0 / math.sqrt(ctx_count * seq_len)
    to_right = [(i, i + 1) for i in range(ctx_count - 1)]
    to_left = [(i + 1, i) for i in range(ctx_count - 1)]

    prior = lax.ppermute(kv_product[:, seq_len - taps :], "ctx", to_right)
    all_filters = lax.all_gather(filters.reshape(chan_count, taps), "ctx", axis=0, tiled=True)
    grad_full = lax.all_gather(out_grad, "fsdp", axis=0, tiled=True)
    w_full = lax.all_gather(w_out, "ctx", axis=0, tiled=True)

    mixed, gated = run_mix(all_filters, kv_product, prior, gate_values)
    w_part = lax.dot_general(
        grad_full, gated, (((1,), (1,)), ((), ())), preferred_element_type=F32
    )
    w_grad = lax.psum_scatter(w_part, "ctx", scatter_dimension=0, tiled=True) * norm_scale

    mix_grad = lax.dot_general(
        w_full, grad_full, (((0,), (0,)), ((), ())), preferred_element_type=F32
    )
    conv_grad = (mix_grad * gate_values.astype(F32)).astype(BF16)
    gate_grad = mix_grad * mixed.astype(F32)
    after = lax.ppermute(conv_grad[:, :taps], "ctx", to_left)
    back = jnp.roll(all_filters[:, ::-1], 1, axis=1)
    kv_grad, filt_part = run_grad(back, conv_grad, after, kv_product)
    filter_grad = lax.psum_scatter(filt_part, "ctx", scatter_dimension=0, tiled=True) * norm_scale
    return (gate_grad, kv_grad, filter_grad.reshape(filters.shape), w_grad)


def solution(mesh):
    in_specs = (
        P("fsdp", "ctx"),
        P("fsdp", "ctx"),
        P("fsdp", "ctx"),
        P("ctx", "fsdp"),
        P("fsdp", "ctx", None, None),
    )
    out_specs = (P("fsdp", "ctx"), P("fsdp", "ctx"), P("fsdp", "ctx", None, None), P("ctx", "fsdp"))
    return jax.shard_map(
        on_device, mesh=mesh, in_specs=in_specs, out_specs=out_specs, check_vma=False
    )
```

time: 1240 us -> 1220 us (0.984); the launches traced: 1220 us -> 1210 us
  waiting for transfers between devices: 472 us -> 812 us
  blocking collectives: 351 us -> 51.2 us
  Pallas kernels: 0 us -> 257 us
  local copies, waits for them, and re-layouts: 254 us -> 19.4 us
  matrix products: 91.7 us -> 46.6 us
    all_to_all x2 -> x0, blocking collectives: 351 us -> none  [the longest x1 210 us: on_device(): lax.all_to_all(mixed.astype(jnp.bfloat16), 'ctx', split_axis=1, concat_ax...]
    reduce_scatter x1 -> x2, waiting for transfers between devices: 424 us -> 733 us  [the longest x1 681 us: on_device(): lax.psum_scatter(w_part, 'ctx', scatter_dimension=0, tiled=True)]
    pallas_call x0 -> x2, Pallas kernels: none -> 257 us  [the longest x1 166 us: run_grad(): pl.pallas_call(grad_kernel, grid=(chan // GROUP,), in_specs=[rows(taps),...]
    reshape x6 -> x0, local copies, waits for them, and re-layouts: 69.1 us -> none  [the longest x4 54.4 us: make_band(): window_cut.reshape(channels, tap_count, 2 * tap_count - 1)[:, :, :tap_count]]
    all_gather x1, waiting for transfers between devices: 0.01 us -> 65 us  [on_device(): w_full = lax.all_gather(w_out, 'ctx', axis=0, tiled=True)]
    all_gather x0 -> x1, blocking collectives: none -> 51.2 us  [on_device(): lax.all_gather(filters.reshape(chan_count, taps), 'ctx', axis=0, tiled=True)]
    pad x4 -> x0, local copies, waits for them, and re-layouts: 49.2 us -> none  [the longest x2 26.9 us: make_band(): window_cut = tiled[:, tap_count:tap_count + tap_count * (2 * tap_count - 1)]]
    unnamed x23 -> x19, local copies, waits for them, and re-layouts: 65 us -> 16.5 us
  transfers between devices with their start and end apart: 5 -> 6, of which waited for: 2 -> 4; matrix products, arithmetic and copies ran while one was open for 25% -> 2% of each run, Pallas kernels for 0% -> 7%
where the time goes in v1:
time: 1220 us; the launch traced here: 1210 us
  waiting for transfers between devices  812 us (67%)
  Pallas kernels  257 us (21%)
  blocking collectives  51.2 us (4%)
  matrix products  46.6 us (4%)
  local copies, waits for them, and re-layouts  19.4 us (2%)
  between operations  13.9 us (1%)
    reduce_scatter x1, waiting for transfers between devices, on_device(): lax.psum_scatter(w_part, 'ctx', scatter_dimension=0, tiled=True)  681 us
    pallas_call x1, Pallas kernels, run_grad(): pl.pallas_call(grad_kernel, grid=(chan // GROUP,), in_specs=[rows(taps),...  166 us
    pallas_call x1, Pallas kernels, run_mix(): pl.pallas_call(mix_kernel, grid=(chan // GROUP,), in_specs=[rows(taps), r...  90.5 us
    all_gather x1, waiting for transfers between devices, on_device(): w_full = lax.all_gather(w_out, 'ctx', axis=0, tiled=True)  65 us
    reduce_scatter x1, waiting for transfers between devices, on_device(): lax.psum_scatter(filt_part, 'ctx', scatter_dimension=0, tiled=True)  52.4 us
    all_gather x1, blocking collectives, on_device(): lax.all_gather(filters.reshape(chan_count, taps), 'ctx', axis=0, tiled=True)  51.2 us
    dot_general x1, matrix products, on_device(): lax.dot_general(grad_full, gated, (((1,), (1,)), ((), ())), preferred_ele...  25.2 us
  transfers between devices with their start and end apart: 6, of which 4 were waited for; matrix products, arithmetic and copies ran while one was open for 2% of the time, Pallas kernels for 7%

profile of v1, /device:TPU:0, one launch (start us, length us, event | category | flops | bytes accessed | tf_op | source)
XLA Modules:
  0.0 1214.3 jit_solution(13942267268587230994)
XLA Ops:
  7.2 0.7 all-gather.6.cloned.1.call-update
  7.9 0.0 all-gather.4.cloned.1.call-start
  7.9 0.7 all-gather.4.cloned.1.call-update
  8.6 0.0 reduce-scatter.3.cloned.1.call-start
  8.7 1.1 slice.18
  9.8 4.9 collective-permute-start
  14.7 51.2 %all-gather = bf16[1,1,2048,128]{3,2,1,0:T(8,128)(2,1)S(1)} all-gather(bf16[1,1,128,128]{3,2,1,0:T(8,128)(2,1)} %param.9), channel_id=2, replica_groups=mesh['ctx'=16,'fsdp'=2] {'ctx'}, dimensions={2}, use_global_device_ids=true | all-gather | bytes 557056 | tf_op jit(solution)/shard_map/all_gather | solution.py:150
  65.9 2.2 copy-done.2
  68.1 2.2 copy-done.4
  70.3 90.5 %mix_kernel.1 = (bf16[2048,1024]{1,0:T(8,128)(2,1)S(1)}, bf16[2048,1024]{1,0:T(8,128)(2,1)S(1)}) custom-call(bf16[2048,128]{1,0:T(8,128)(2,1)S(1)} %bitcast.10, bf16[2048,1024]{1,0:T(8,128)(2,1)S(1)} %copy-done.2, bf16[2048,128]{1,0:T(8,128)(2,1)S(1)} %collective-permute-done.prior_ref, bf16[2048,1024]{1,0:T(8,128)(2,1)S(1)} %copy-done.4), custom_call_target="tpu_custom_call" | custom-call | tf_op jit(solution)/shard_map/mix_kernel/pallas_call | solution.py:65
  160.8 2.0 copy-done.6
  162.8 1.9 copy-done.8
  164.7 65.0 %all-gather.4.cloned.1.call-done = bf16[4096,2048]{1,0:T(8,128)(2,1)} async-done(((bf16[256,2048]{1,0:T(8,128)(2,1)}), bf16[4096,2048]{1,0:T(8,128)(2,1)}) %all-gather.4.cloned.1.call-update) | async-done | bytes 16777232 | tf_op jit(solution)/shard_map/all_gather | solution.py:152
  229.7 21.5 %fusion = f32[2048,1024]{1,0:T(8,128)S(1)} fusion(bf16[4096,2048]{1,0:T(8,128)(2,1)} %all-gather.4.cloned.1.call-done, bf16[4096,1024]{1,0:T(8,128)(2,1)} %all-gather.6.cloned.1.call-done), kind=kOutput, calls=%fused_computation.6 | convolution fusion | flops 17179869184 | bytes 33554432 | tf_op jit(solution)/shard_map/dot_general | solution.py:160
  251.2 4.7 multiply_convert_fusion
  255.9 0.1 slice.25
  256.1 2.0 copy-done
  258.1 1.3 collective-permute-start.1
  259.3 0.2 slice.24
  259.6 1.5 slice.21
  261.0 0.3 pad_maximum_fusion.back_ref
  261.3 11.9 collective-permute-done.1.after_ref
  273.2 2.2 copy-done.1
  275.4 2.2 copy-done.3
  277.6 166.3 %grad_kernel.1 = (bf16[2048,1024]{1,0:T(8,128)(2,1)}, f32[2048,128]{1,0:T(8,128)}) custom-call(bf16[2048,128]{1,0:T(8,128)(2,1)S(1)} %pad_maximum_fusion.back_ref, bf16[2048,1024]{1,0:T(8,128)(2,1)S(1)} %copy-done.1, bf16[2048,128]{1,0:T(8,128)(2,1)S(1)} %collective-permute-done.1.after_ref, bf16[2048,1024]{1,0:T(8,128)(2,1)S(1)} %copy-done.3), custom_call_target="tpu_custom_call" | custom-call | tf_op jit(solution)/shard_map/grad_kernel/pallas_call | solution.py:124
  443.9 0.2 reduce-scatter.5.cloned.1.call-start
  444.1 25.2 %convolution_bitcast_fusion = f32[4096,2048]{0,1:T(8,128)} fusion(bf16[2048,1024]{1,0:T(8,128)(2,1)} %copy-done.8, bf16[4096,1024]{1,0:T(8,128)(2,1)} %all-gather.6.cloned.1.call-done), kind=kOutput, calls=%fused_computation | convolution fusion | flops 17179869184 | bytes 46137344 | tf_op jit(solution)/shard_map/dot_general | solution.py:155
  469.3 52.4 %reduce-scatter.3.cloned.1.call-done = f32[128,128]{1,0:T(8,128)} async-done(((f32[2048,128]{1,0:T(8,128)}), f32[128,128]{1,0:T(8,128)}) %reduce-scatter.3.cloned.1.call-update) | async-done | bytes 65552 | tf_op jit(solution)/shard_map/reduce_scatter | solution.py:168
  521.7 1.5 multiply_bitcast_fusion
  523.2 681.0 %reduce-scatter.5.cloned.1.call-done = f32[256,2048]{0,1:T(8,128)} async-done(((f32[4096,2048]{0,1:T(8,128)}), f32[256,2048]{0,1:T(8,128)}) %reduce-scatter.5.cloned.1.call-update) | async-done | bytes 2097168 | tf_op jit(solution)/shard_map/reduce_scatter | solution.py:158
  1204.2 1.7 broadcast_multiply_fusion
  1205.9 1.8 copy.9
  (16 shorter events, 0.1 us)
Async XLA Ops:
  7.2 157.5 %all-gather.6.cloned.1.call-start = ((), (), s32[]{:S(2)}) async-start(), calls=%async_computation.3 | async-start | bytes 12582912 | tf_op jit(solution)/shard_map/all_gather | solution.py:151
  7.9 221.8 %all-gather.4.cloned.1.call-start = ((), (), s32[]{:S(2)}) async-start(), calls=%async_computation.2 | async-start | bytes 17825792 | tf_op jit(solution)/shard_map/all_gather | solution.py:152
  8.6 513.1 %reduce-scatter.3.cloned.1.call-start = ((), (), s32[]{:S(2)}) async-start(), calls=%async_computation.4 | async-start | bytes 1114112 | tf_op jit(solution)/shard_map/reduce_scatter | solution.py:168
  9.8 56.1 %collective-permute-start = (bf16[2048,128]{1,0:T(8,128)(2,1)S(1)}, bf16[2048,128]{1,0:T(8,128)(2,1)S(1)}, u32[]{:S(2)}, u32[]{:S(2)}) collective-permute-start(bf16[2048,128]{1,0:T(8,128)(2,1)S(1)} %slice.18), channel_id=1, source_target_pairs={{0,2},{2,4},{4,6},{6,8},{8,10},{10,12},{12,14},{14,16},{16,18},{18... | collective-permute-start | bytes 1572872 | tf_op jit(solution)/shard_map/ppermute | solution.py:149
  65.9 2.2 copy-start.2
  68.1 2.2 copy-start.4
  160.8 2.0 copy-start.6
  162.8 1.9 copy-start.8
  229.7 21.5 %copy-start.5 = (bf16[2048,1024]{1,0:T(8,128)(2,1)S(1)}, bf16[2048,1024]{1,0:T(8,128)(2,1)}, u32[]{:S(2)}) copy-start(bf16[2048,1024]{1,0:T(8,128)(2,1)} %gate_ref.1) | copy-start | bytes 12582916
  229.7 21.5 %copy-start.7 = (bf16[2048,1024]{1,0:T(8,128)(2,1)S(1)}, bf16[2048,1024]{1,0:T(8,128)(2,1)}, u32[]{:S(2)}) copy-start(bf16[2048,1024]{1,0:T(8,128)(2,1)} %copy-done.6) | copy-start | bytes 12582916
  256.0 2.0 copy-start
  258.1 15.2 %collective-permute-start.1 = (bf16[2048,128]{1,0:T(8,128)(2,1)S(1)}, bf16[2048,128]{1,0:T(8,128)(2,1)S(1)}, u32[]{:S(2)}, u32[]{:S(2)}) collective-permute-start(bf16[2048,128]{1,0:T(8,128)(2,1)S(1)} %slice.25), channel_id=1, source_target_pairs={{2,0},{4,2},{6,4},{8,6},{10,8},{12,10},{14,12},{16,14},{18,16},{20... | collective-permute-start | bytes 1572872 | tf_op jit(solution)/shard_map/ppermute | solution.py:165
  273.2 2.2 copy-start.1
  275.4 2.2 copy-start.3
  443.9 760.3 %reduce-scatter.5.cloned.1.call-start = ((), (), s32[]{:S(2)}) async-start(), calls=%async_computation.5 | async-start | bytes 35651584 | tf_op jit(solution)/shard_map/reduce_scatter | solution.py:158
Sparse Core Ops, SparseCore 0:
  9.5 22.5 all-gather.5
  34.9 194.7 all-gather.3
  444.0 77.6 reduce-scatter.2
  524.0 680.0 reduce-scatter.4

commit v2 on v1

v2 whole, which is shorter than its diff:
```python
import math

import jax
import jax.numpy as jnp
import ml_dtypes
import numpy as np
from jax import lax
from jax.experimental import pallas as pl
from jax.experimental.pallas import tpu as pltpu
from jax.sharding import PartitionSpec as P

F32 = jnp.float32
BF16 = jnp.bfloat16
MIB = 1024 * 1024


def split_pair(matrix):
    high = matrix.astype(ml_dtypes.bfloat16)
    low = (matrix - high.astype(np.float64)).astype(ml_dtypes.bfloat16)
    return high, low


def dft_matrices(taps):
    points = 2 * taps
    place = np.arange(taps)
    angle = 2.0 * np.pi * ((place[:, None] * place[None, :]) % points) / points
    turn = (-1.0) ** place
    forward = np.concatenate([np.cos(angle), -np.sin(angle)], axis=1)
    forward[:, taps] = turn
    weight = np.full((taps, 1), 2.0 / points)
    weight[0] = 1.0 / points
    backward = np.concatenate([weight * np.cos(angle), -weight * np.sin(angle)], axis=0)
    backward[taps, :] = turn / points
    forward = np.concatenate(split_pair(forward), axis=0)
    backward = np.concatenate(split_pair(backward), axis=1)
    return forward, backward


def spectrum(block, forward):
    taps = block.shape[1]
    both = jnp.dot(jnp.concatenate([block, block], axis=1), forward, preferred_element_type=F32)
    return both[:, :taps], both[:, taps:]


def inverse(real, imag, backward):
    taps = real.shape[1]
    whole = jnp.concatenate([real, imag], axis=1)
    high = whole.astype(BF16)
    low = (whole - high.astype(F32)).astype(BF16)
    both = jnp.dot(high, backward, preferred_element_type=F32)
    rest = jnp.dot(low, backward[:, :taps], preferred_element_type=F32)
    return both[:, :taps] + both[:, taps:] + rest


def lane_facts(taps):
    lane = lax.broadcasted_iota(jnp.int32, (1, taps), 1)
    sign = jnp.where(lane % 2 == 0, 1.0, -1.0)
    return lane == 0, sign


def filter_spectrum(filt, forward, first):
    real, imag = spectrum(filt, forward)
    return real, jnp.where(first, imag, real), jnp.where(first, 0.0, imag)


def mix_kernel(filt_ref, kv_ref, prior_ref, gate_ref, forward_ref, backward_ref, mixed_ref, gated_ref):
    taps = filt_ref.shape[1]
    blocks = kv_ref.shape[1] // taps
    forward, backward = forward_ref[...], backward_ref[...]
    first, sign = lane_facts(taps)
    sign_imag = jnp.where(first, 1.0, sign)
    h_real, h_last, h_imag = filter_spectrum(filt_ref[...], forward, first)
    prev_real, prev_imag = spectrum(prior_ref[...], forward)
    for b in range(blocks):
        span = slice(b * taps, (b + 1) * taps)
        real, imag = spectrum(kv_ref[:, span], forward)
        win_real = real + sign * prev_real
        win_imag = imag + sign_imag * prev_imag
        mixed = inverse(
            h_real * win_real - h_imag * win_imag, h_last * win_imag + h_imag * win_real, backward
        ).astype(BF16)
        mixed_ref[:, span] = mixed
        gated_ref[:, span] = (gate_ref[:, span].astype(F32) * mixed.astype(F32)).astype(BF16)
        prev_real, prev_imag = real, imag


def run_mix(filters, kv, prior, gate, forward, backward):
    chan, seq_len = kv.shape
    taps = filters.shape[1]
    group = min(256, chan)
    rows = lambda width: pl.BlockSpec((group, width), lambda g: (g, 0))
    whole = lambda array: pl.BlockSpec(array.shape, lambda g: (0, 0))
    return pl.pallas_call(
        mix_kernel,
        grid=(chan // group,),
        in_specs=[rows(taps), rows(seq_len), rows(taps), rows(seq_len), whole(forward), whole(backward)],
        out_specs=[rows(seq_len), rows(seq_len)],
        out_shape=[jax.ShapeDtypeStruct((chan, seq_len), BF16)] * 2,
        compiler_params=pltpu.CompilerParams(vmem_limit_bytes=32 * MIB),
        name="mix_kernel",
    )(filters, kv, prior, gate, forward, backward)


def grad_kernel(
    filt_ref, grad_ref, after_ref, kv_ref, forward_ref, backward_ref, kv_grad_ref, filt_grad_ref
):
    taps = filt_ref.shape[1]
    blocks = kv_ref.shape[1] // taps
    forward, backward = forward_ref[...], backward_ref[...]
    first, sign = lane_facts(taps)
    sign_imag = jnp.where(first, 1.0, sign)
    h_real, h_last, h_imag = filter_spectrum(filt_ref[...], forward, first)
    total_real = total_imag = None
    next_real, next_imag = spectrum(after_ref[...], forward)
    for b in reversed(range(blocks)):
        span = slice(b * taps, (b + 1) * taps)
        real, imag = spectrum(grad_ref[:, span], forward)
        win_real = real + sign * next_real
        win_imag = imag + sign_imag * next_imag
        kv_grad_ref[:, span] = inverse(
            h_real * win_real + h_imag * win_imag, h_last * win_imag - h_imag * win_real, backward
        ).astype(BF16)
        x_real, x_last, x_imag = filter_spectrum(kv_ref[:, span], forward, first)
        part_real = x_real * win_real + x_imag * win_imag
        part_imag = x_last * win_imag - x_imag * win_real
        total_real = part_real if total_real is None else total_real + part_real
        total_imag = part_imag if total_imag is None else total_imag + part_imag
        next_real, next_imag = real, imag
    filt_grad_ref[...] = inverse(total_real, total_imag, backward)


def run_grad(filters, grad, after, kv, forward, backward):
    chan, seq_len = kv.shape
    taps = filters.shape[1]
    group = min(256, chan)
    rows = lambda width: pl.BlockSpec((group, width), lambda g: (g, 0))
    whole = lambda array: pl.BlockSpec(array.shape, lambda g: (0, 0))
    return pl.pallas_call(
        grad_kernel,
        grid=(chan // group,),
        in_specs=[rows(taps), rows(seq_len), rows(taps), rows(seq_len), whole(forward), whole(backward)],
        out_specs=[rows(seq_len), rows(taps)],
        out_shape=[
            jax.ShapeDtypeStruct((chan, seq_len), BF16),
            jax.ShapeDtypeStruct((chan, taps), F32),
        ],
        compiler_params=pltpu.CompilerParams(vmem_limit_bytes=32 * MIB),
        name="grad_kernel",
    )(filters, grad, after, kv, forward, backward)


def weight_kernel(place_ref, g00, g01, g10, g11, left_ref, right_ref, send_a, keep_a, send_b, keep_b):
    rows = g00.shape[0]
    stack = jnp.concatenate([g01[...], g11[...], g00[...], g10[...]], axis=0)
    contract = (((1,), (1,)), ((), ()))
    left = lax.dot_general(stack, left_ref[...], contract, preferred_element_type=F32).astype(BF16)
    send_a[0] = left[:rows]
    send_a[1] = left[rows : 2 * rows]
    keep_a[0] = left[2 * rows : 3 * rows]
    keep_a[1] = left[3 * rows :]
    right = lax.dot_general(stack, right_ref[...], contract, preferred_element_type=F32).astype(BF16)
    send_b[0] = right[3 * rows :]
    send_b[1] = right[rows : 2 * rows]
    keep_b[0] = right[2 * rows : 3 * rows]
    keep_b[1] = right[:rows]


def run_weight(place, grad_full, gated, rows):
    chan, seq_len = gated.shape
    width = chan // 4
    grad_spec = lambda k: pl.BlockSpec((rows, seq_len), lambda n, place: (place[k], 0))
    gated_spec = lambda first: pl.BlockSpec((width, seq_len), lambda n, place: (n + first, 0))
    out_spec = pl.BlockSpec((2, rows, width), lambda n, place: (0, 0, n))
    return pl.pallas_call(
        weight_kernel,
        grid_spec=pltpu.PrefetchScalarGridSpec(
            num_scalar_prefetch=1,
            grid=(2,),
            in_specs=[grad_spec(k) for k in range(4)] + [gated_spec(0), gated_spec(2)],
            out_specs=[out_spec] * 4,
        ),
        out_shape=[jax.ShapeDtypeStruct((2, rows, chan // 2), BF16)] * 4,
        compiler_params=pltpu.CompilerParams(vmem_limit_bytes=48 * MIB),
        name="weight_kernel",
    )(place, grad_full, grad_full, grad_full, grad_full, gated, gated)


class Layout:
    def __init__(self):
        self.count = lax.axis_size("ctx")
        self.depth = self.count // 4
        index = lax.axis_index("ctx")
        self.z, self.y, self.x = index // 4, (index // 2) % 2, index % 2

    def swap_x(self, array):
        return lax.ppermute(array, "ctx", [(i, i ^ 1) for i in range(self.count)])

    def swap_y(self, array):
        return lax.ppermute(array, "ctx", [(i, i ^ 2) for i in range(self.count)])

    def shift_z(self, array, by):
        return lax.ppermute(array, "ctx", [(i, (i + 4 * by) % self.count) for i in range(self.count)])


def pick(bit, array, axis):
    halves = [lax.index_in_dim(array, k, axis, keepdims=False) for k in range(2)]
    return jnp.where(bit == 0, halves[0], halves[1])


def gather_filters(at, own):
    def ordered(bit, mine, other):
        return jnp.stack([jnp.where(bit == 0, mine, other), jnp.where(bit == 0, other, mine)])

    pair = ordered(at.x, own, at.swap_x(own))
    plane = ordered(at.y, pair, at.swap_y(pair))
    slots = [at.shift_z(plane, by) for by in range(at.depth - 1, 0, -1)] + [plane]
    ring = jnp.stack(slots + slots)
    whole = lax.dynamic_slice_in_dim(ring, at.depth - 1 - at.z, at.depth, axis=0)
    return whole.reshape((at.count * own.shape[0],) + own.shape[1:])


def reduce_filters(at, part, chan_count):
    taps = part.shape[1]
    part = part.reshape(at.depth, 2, 2, chan_count, taps)
    part = pick(at.x, part, 2) + at.swap_x(pick(1 - at.x, part, 2))
    part = pick(at.y, part, 1) + at.swap_y(pick(1 - at.y, part, 1))
    at_z = lambda by: lax.dynamic_index_in_dim(part, (at.z + by) % at.depth, 0, keepdims=False)
    total = at_z(0)
    for by in range(1, at.depth):
        total = total + at.shift_z(at_z(by), by)
    return total


def reduce_weight(at, grad_full, gated, rows):
    total = None
    received = []
    for by in sorted(range(at.depth), key=lambda d: -min(d, at.depth - d)):
        base = 4 * ((at.z + by) % at.depth)
        place = jnp.stack(
            [base + 2 * (at.y ^ dy) + (at.x ^ dx) for dy in range(2) for dx in range(2)]
        ).astype(jnp.int32)
        send_a, keep_a, send_b, keep_b = run_weight(place, grad_full, gated, rows)
        got_a, got_b = at.swap_x(send_a), at.swap_y(send_b)
        next_a = (keep_a[1].astype(F32) + got_a[1].astype(F32)).astype(BF16)
        next_b = (keep_b[1].astype(F32) + got_b[1].astype(F32)).astype(BF16)
        last_a, last_b = at.swap_y(next_a), at.swap_x(next_b)
        sum_a = keep_a[0].astype(F32) + got_a[0].astype(F32) + last_a.astype(F32)
        sum_b = keep_b[0].astype(F32) + got_b[0].astype(F32) + last_b.astype(F32)
        joint = jnp.concatenate([sum_a, sum_b], axis=1)
        if by == 0:
            total = joint
        else:
            received.append(at.shift_z(joint.astype(BF16), by))
    for piece in received:
        total = total + piece.astype(F32)
    return total


def on_device(out_grad, gate_values, kv_product, w_out, filters):
    at = Layout()
    chan_count = filters.shape[2]
    taps = filters.shape[3]
    seq_len = out_grad.shape[1]
    norm_scale = 1.0 / math.sqrt(at.count * seq_len)
    to_right = [(i, i + 1) for i in range(at.count - 1)]
    to_left = [(i + 1, i) for i in range(at.count - 1)]
    forward, backward = (jnp.asarray(m) for m in dft_matrices(taps))

    prior = lax.ppermute(kv_product[:, seq_len - taps :], "ctx", to_right)
    all_filters = gather_filters(at, filters.reshape(chan_count, taps))
    grad_full = lax.all_gather(out_grad, "fsdp", axis=0, tiled=True)
    w_full = lax.all_gather(w_out, "ctx", axis=0, tiled=True)

    mixed, gated = run_mix(all_filters, kv_product, prior, gate_values, forward, backward)
    w_grad = reduce_weight(at, grad_full, gated, w_out.shape[0]) * norm_scale

    mix_grad = lax.dot_general(
        w_full, grad_full, (((0,), (0,)), ((), ())), preferred_element_type=F32
    )
    conv_grad = (mix_grad * gate_values.astype(F32)).astype(BF16)
    gate_grad = mix_grad * mixed.astype(F32)
    after = lax.ppermute(conv_grad[:, :taps], "ctx", to_left)
    kv_grad, filt_part = run_grad(all_filters, conv_grad, after, kv_product, forward, backward)
    filter_grad = reduce_filters(at, filt_part, chan_count) * norm_scale
    return (gate_grad, kv_grad, filter_grad.reshape(filters.shape), w_grad)


def solution(mesh):
    in_specs = (
        P("fsdp", "ctx"),
        P("fsdp", "ctx"),
        P("fsdp", "ctx"),
        P("ctx", "fsdp"),
        P("fsdp", "ctx", None, None),
    )
    out_specs = (P("fsdp", "ctx"), P("fsdp", "ctx"), P("fsdp", "ctx", None, None), P("ctx", "fsdp"))
    return jax.shard_map(
        on_device, mesh=mesh, in_specs=in_specs, out_specs=out_specs, check_vma=False
    )
```

time: 1220 us -> 464 us (0.38)
  waiting for transfers between devices: 812 us -> 246 us
  Pallas kernels: 257 us -> 68.1 us
  starting transfers between devices: 6.49 us -> 73.2 us
  blocking collectives: 51.2 us -> 0 us
  matrix products: 46.6 us -> 21.5 us
  other arithmetic: 8.22 us -> 27.7 us
    reduce_scatter x2 -> x0, waiting for transfers between devices: 733 us -> none  [the longest x1 681 us: on_device(): lax.psum_scatter(w_part, 'ctx', scatter_dimension=0, tiled=True)]
    ppermute x0 -> x29, waiting for transfers between devices: none -> 201 us  [the longest x10 145 us: swap_x(): return lax.ppermute(array, 'ctx', [(i, i ^ 1) for i in range(self.count)])]
    pallas_call x2 -> x6, Pallas kernels: 257 us -> 68.1 us  [the longest x4 32.7 us: run_weight(): pl.pallas_call(weight_kernel, grid_spec=pltpu.PrefetchScalarGridSpec(num_...]
    ppermute x0 -> x29, starting transfers between devices: none -> 68.2 us  [the longest x10 29.6 us: swap_x(): return lax.ppermute(array, 'ctx', [(i, i ^ 1) for i in range(self.count)])]
    all_gather x1 -> x0, blocking collectives: 51.2 us -> none  [on_device(): lax.all_gather(filters.reshape(chan_count, taps), 'ctx', axis=0, tiled=True)]
    all_gather x1, waiting for transfers between devices: 65 us -> 34.8 us  [on_device(): w_full = lax.all_gather(w_out, 'ctx', axis=0, tiled=True)]
    dot_general x1 -> x0, matrix products: 25.2 us -> none  [on_device(): lax.dot_general(grad_full, gated, (((1,), (1,)), ((), ())), preferred_ele...]
  transfers between devices with their start and end apart: 6 -> 33, of which waited for: 4 -> 19; matrix products, arithmetic and copies ran while one was open for 2% -> 11% of each run, Pallas kernels for 7% -> 15%
where the time goes in v2:
time: 464 us; the launch traced here: 463 us
  waiting for transfers between devices  246 us (53%)
  starting transfers between devices  73.2 us (16%)
  Pallas kernels  68.1 us (15%)
  other arithmetic  27.7 us (6%)
  matrix products  21.5 us (5%)
  between operations  14.6 us (3%)
  local copies, waits for them, and re-layouts  11.9 us (3%)
    ppermute x10, waiting for transfers between devices, swap_x(): return lax.ppermute(array, 'ctx', [(i, i ^ 1) for i in range(self.count)])  145 us
    ppermute x9, waiting for transfers between devices, shift_z(): lax.ppermute(array, 'ctx', [(i, (i + 4 * by) % self.count) for i in range...  36.2 us
    all_gather x1, waiting for transfers between devices, on_device(): w_full = lax.all_gather(w_out, 'ctx', axis=0, tiled=True)  34.8 us
    pallas_call x4, Pallas kernels, run_weight(): pl.pallas_call(weight_kernel, grid_spec=pltpu.PrefetchScalarGridSpec(num_...  32.7 us
    ppermute x10, starting transfers between devices, swap_x(): return lax.ppermute(array, 'ctx', [(i, i ^ 1) for i in range(self.count)])  29.6 us
    ppermute x9, starting transfers between devices, shift_z(): lax.ppermute(array, 'ctx', [(i, (i + 4 * by) % self.count) for i in range...  22.9 us
    dot_general x1, matrix products, on_device(): lax.dot_general(w_full, grad_full, (((0,), (0,)), ((), ())), preferred_el...  21.5 us
    ppermute x10, waiting for transfers between devices, swap_y(): return lax.ppermute(array, 'ctx', [(i, i ^ 2) for i in range(self.count)])  20.2 us
  transfers between devices with their start and end apart: 33, of which 19 were waited for; matrix products, arithmetic and copies ran while one was open for 11% of the time, Pallas kernels for 15%

profile of v2, /device:TPU:0, one launch (start us, length us, event | category | flops | bytes accessed | tf_op | source)
XLA Modules:
  0.0 463.4 jit_solution(16980260917517892114)
XLA Ops:
  18.0 4.2 collective-permute-start.2
  23.4 3.4 collective-permute-start.5
  27.9 6.5 %collective-permute-done.3 = bf16[2,2,128,128]{3,2,1,0:T(8,128)(2,1)S(1)} collective-permute-done((bf16[2,2,128,128]{3,2,1,0:T(8,128)(2,1)S(1)}, bf16[2,2,128,128]{3,2,1,0:T(8,128)(2,1)S(1)}, u32[]{:S(2)}, u32[]{:S(2)}) %collective-permute-start.3) | collective-permute-done | bytes 131104 | tf_op jit(solution)/shard_map/ppermute | solution.py:202
  39.7 15.9 %mix_kernel.1 = (bf16[2048,1024]{1,0:T(8,128)(2,1)S(1)}, bf16[2048,1024]{1,0:T(8,128)(2,1)S(1)}) custom-call(bf16[2048,128]{1,0:T(8,128)(2,1)S(1)} %bitcast.137, bf16[2048,1024]{1,0:T(8,128)(2,1)S(1)} %copy-done.1, bf16[2048,128]{1,0:T(8,128)(2,1)S(1)} %collective-permute-done.5.prior_ref, bf16[2048,1024]{1,0:T(8,128)(2,1)S(1)} %copy-done.3, ...), custom_call_target="tpu_custom_call" | custom-call | tf_op jit(solution)/shard_map/mix_kernel/pallas_call | solution.py:93
  59.7 8.4 %weight_kernel.4 = (bf16[2,256,1024]{2,1,0:T(8,128)(2,1)}, bf16[2,256,1024]{2,1,0:T(8,128)(2,1)S(1)}, bf16[2,256,1024]{2,1,0:T(8,128)(2,1)}, bf16[2,256,1024]{2,1,0:T(8,128)(2,1)S(1)}) custom-call(s32[4]{0:T(128)S(1)} %get-tuple-element.53.place_ref, bf16[4096,1024]{1,0:T(8,128)(2,1)} %all-gather.5.cloned.1.call-done.g00.g01.g10.g11, ...), custom_call_target="tpu_custom_call" | custom-call | tf_op jit(solution)/shard_map/weight_kernel/pallas_call | solution.py:174
  68.1 3.4 collective-permute-start.14
  71.5 6.2 %collective-permute-start.12 = (bf16[2,256,1024]{2,1,0:T(8,128)(2,1)}, bf16[2,256,1024]{2,1,0:T(8,128)(2,1)}, u32[]{:S(2)}, u32[]{:S(2)}) collective-permute-start(bf16[2,256,1024]{2,1,0:T(8,128)(2,1)} %get-tuple-element.29), channel_id=1, source_target_pairs={{0,2},{2,0},{4,6},{6,4},{8,10},{10,8},{12,14},{14,12},{16,18},{18,... | collective-permute-start | bytes 3145736 | tf_op jit(solution)/shard_map/ppermute | solution.py:196
  77.8 8.4 %weight_kernel.7 = (bf16[2,256,1024]{2,1,0:T(8,128)(2,1)}, bf16[2,256,1024]{2,1,0:T(8,128)(2,1)S(1)}, bf16[2,256,1024]{2,1,0:T(8,128)(2,1)}, bf16[2,256,1024]{2,1,0:T(8,128)(2,1)S(1)}) custom-call(s32[4]{0:T(128)S(1)} %get-tuple-element.56.place_ref, bf16[4096,1024]{1,0:T(8,128)(2,1)} %all-gather.5.cloned.1.call-done.g00.g01.g10.g11, ...), custom_call_target="tpu_custom_call" | custom-call | tf_op jit(solution)/shard_map/weight_kernel/pallas_call | solution.py:174
  88.9 7.8 %weight_kernel.6 = (bf16[2,256,1024]{2,1,0:T(8,128)(2,1)S(1)}, bf16[2,256,1024]{2,1,0:T(8,128)(2,1)S(1)}, bf16[2,256,1024]{2,1,0:T(8,128)(2,1)S(1)}, bf16[2,256,1024]{2,1,0:T(8,128)(2,1)S(1)}) custom-call(s32[4]{0:T(128)S(1)} %get-tuple-element.55.place_ref, bf16[4096,1024]{1,0:T(8,128)(2,1)} %all-gather.5.cloned.1.call-done.g00.g01.g10.g11, ...), custom_call_target="tpu_custom_call" | custom-call | tf_op jit(solution)/shard_map/weight_kernel/pallas_call | solution.py:174
  98.6 8.0 %weight_kernel.5 = (bf16[2,256,1024]{2,1,0:T(8,128)(2,1)S(1)}, bf16[2,256,1024]{2,1,0:T(8,128)(2,1)S(1)}, bf16[2,256,1024]{2,1,0:T(8,128)(2,1)S(1)}, bf16[2,256,1024]{2,1,0:T(8,128)(2,1)S(1)}) custom-call(s32[4]{0:T(128)S(1)} %get-tuple-element.54.place_ref, bf16[4096,1024]{1,0:T(8,128)(2,1)} %all-gather.5.cloned.1.call-done.g00.g01.g10.g11, ...), custom_call_target="tpu_custom_call" | custom-call | tf_op jit(solution)/shard_map/weight_kernel/pallas_call | solution.py:174
  106.7 4.3 collective-permute-done.14
  110.9 6.2 %collective-permute-start.21 = (bf16[2,256,1024]{2,1,0:T(8,128)(2,1)S(1)}, bf16[2,256,1024]{2,1,0:T(8,128)(2,1)S(1)}, u32[]{:S(2)}, u32[]{:S(2)}) collective-permute-start(bf16[2,256,1024]{2,1,0:T(8,128)(2,1)S(1)} %get-tuple-element.37), channel_id=1, source_target_pairs={{0,2},{2,0},{4,6},{6,4},{8,10},{10,8},{12,14},{14,12},{16,18},{18,... | collective-permute-start | bytes 3145736 | tf_op jit(solution)/shard_map/ppermute | solution.py:196
  119.1 4.9 %collective-permute-done.12 = bf16[2,256,1024]{2,1,0:T(8,128)(2,1)} collective-permute-done((bf16[2,256,1024]{2,1,0:T(8,128)(2,1)}, bf16[2,256,1024]{2,1,0:T(8,128)(2,1)}, u32[]{:S(2)}, u32[]{:S(2)}) %collective-permute-start.12) | collective-permute-done | bytes 1048608 | tf_op jit(solution)/shard_map/ppermute | solution.py:196
  126.0 7.4 %collective-permute-done.28 = bf16[2,256,1024]{2,1,0:T(8,128)(2,1)} collective-permute-done((bf16[2,256,1024]{2,1,0:T(8,128)(2,1)}, bf16[2,256,1024]{2,1,0:T(8,128)(2,1)}, u32[]{:S(2)}, u32[]{:S(2)}) %collective-permute-start.28) | collective-permute-done | bytes 1048608 | tf_op jit(solution)/shard_map/ppermute | solution.py:199
  133.4 6.2 %collective-permute-start.16 = (bf16[2,256,1024]{2,1,0:T(8,128)(2,1)S(1)}, bf16[2,256,1024]{2,1,0:T(8,128)(2,1)S(1)}, u32[]{:S(2)}, u32[]{:S(2)}) collective-permute-start(bf16[2,256,1024]{2,1,0:T(8,128)(2,1)S(1)} %get-tuple-element.33), channel_id=1, source_target_pairs={{0,2},{2,0},{4,6},{6,4},{8,10},{10,8},{12,14},{14,12},{16,18},{18,... | collective-permute-start | bytes 3145736 | tf_op jit(solution)/shard_map/ppermute | solution.py:196
  140.9 13.0 %collective-permute-done.26 = bf16[2,256,1024]{2,1,0:T(8,128)(2,1)} collective-permute-done((bf16[2,256,1024]{2,1,0:T(8,128)(2,1)}, bf16[2,256,1024]{2,1,0:T(8,128)(2,1)}, u32[]{:S(2)}, u32[]{:S(2)}) %collective-permute-start.26) | collective-permute-done | bytes 1048608 | tf_op jit(solution)/shard_map/ppermute | solution.py:196
  158.0 30.5 %collective-permute-done.21 = bf16[2,256,1024]{2,1,0:T(8,128)(2,1)S(1)} collective-permute-done((bf16[2,256,1024]{2,1,0:T(8,128)(2,1)S(1)}, bf16[2,256,1024]{2,1,0:T(8,128)(2,1)S(1)}, u32[]{:S(2)}, u32[]{:S(2)}) %collective-permute-start.21) | collective-permute-done | bytes 1048608 | tf_op jit(solution)/shard_map/ppermute | solution.py:196
  190.5 3.3 collective-permute-done.18
  196.5 37.0 %collective-permute-done.16 = bf16[2,256,1024]{2,1,0:T(8,128)(2,1)S(1)} collective-permute-done((bf16[2,256,1024]{2,1,0:T(8,128)(2,1)S(1)}, bf16[2,256,1024]{2,1,0:T(8,128)(2,1)S(1)}, u32[]{:S(2)}, u32[]{:S(2)}) %collective-permute-start.16) | collective-permute-done | bytes 1048608 | tf_op jit(solution)/shard_map/ppermute | solution.py:196
  236.2 42.2 %collective-permute-done.29 = bf16[256,1024]{1,0:T(8,128)(2,1)S(1)} collective-permute-done((bf16[256,1024]{1,0:T(8,128)(2,1)S(1)}, bf16[256,1024]{1,0:T(8,128)(2,1)S(1)}, u32[]{:S(2)}, u32[]{:S(2)}) %collective-permute-start.29) | collective-permute-done | bytes 524320 | tf_op jit(solution)/shard_map/ppermute | solution.py:196
  283.1 9.1 %collective-permute-done.24 = bf16[256,1024]{1,0:T(8,128)(2,1)S(1)} collective-permute-done((bf16[256,1024]{1,0:T(8,128)(2,1)S(1)}, bf16[256,1024]{1,0:T(8,128)(2,1)S(1)}, u32[]{:S(2)}, u32[]{:S(2)}) %collective-permute-start.24) | collective-permute-done | bytes 524320 | tf_op jit(solution)/shard_map/ppermute | solution.py:196
  300.9 34.8 %all-gather.3.cloned.1.call-done = bf16[4096,2048]{1,0:T(8,128)(2,1)} async-done(((bf16[256,2048]{1,0:T(8,128)(2,1)}), bf16[4096,2048]{1,0:T(8,128)(2,1)}) %all-gather.3.cloned.1.call-update) | async-done | bytes 16777232 | tf_op jit(solution)/shard_map/all_gather | solution.py:272
  335.7 21.5 %fusion.25 = f32[2048,1024]{1,0:T(8,128)S(1)} fusion(bf16[4096,2048]{1,0:T(8,128)(2,1)} %all-gather.3.cloned.1.call-done, bf16[4096,1024]{1,0:T(8,128)(2,1)} %all-gather.5.cloned.1.call-done.g00.g01.g10.g11), kind=kOutput, calls=%fused_computation.74 | convolution fusion | flops 17179869184 | bytes 33554432 | tf_op jit(solution)/shard_map/dot_general | solution.py:277
  357.2 4.7 %multiply_convert_fusion = (bf16[2048,1024]{1,0:T(8,128)(2,1)S(1)}, f32[2048,1024]{1,0:T(8,128)}) fusion(f32[2048,1024]{1,0:T(8,128)S(1)} %fusion.25, bf16[2048,1024]{1,0:T(8,128)(2,1)S(1)} %copy-done.4, bf16[2048,1024]{1,0:T(8,128)(2,1)S(1)} %copy-done.6), kind=kLoop, calls=%fused_computation | loop fusion | flops 10485760 | bytes 29360128 | tf_op jit(solution)/shard_map/convert_element_type | solution.py:280
  363.8 3.7 collective-permute-start.25
  368.9 8.5 %collective-permute-done.6.after_ref = bf16[2048,128]{1,0:T(8,128)(2,1)S(1)} collective-permute-done((bf16[2048,128]{1,0:T(8,128)(2,1)S(1)}, bf16[2048,128]{1,0:T(8,128)(2,1)S(1)}, u32[]{:S(2)}, u32[]{:S(2)}) %collective-permute-start.6) | collective-permute-done | bytes 524320 | tf_op jit(solution)/shard_map/ppermute | solution.py:282
  377.4 19.5 %grad_kernel.1 = (bf16[2048,1024]{1,0:T(8,128)(2,1)}, f32[2048,128]{1,0:T(8,128)S(1)}) custom-call(bf16[2048,128]{1,0:T(8,128)(2,1)S(1)} %bitcast.138, bf16[2048,1024]{1,0:T(8,128)(2,1)S(1)} %get-tuple-element.44.grad_ref, bf16[2048,128]{1,0:T(8,128)(2,1)S(1)} %collective-permute-done.6.after_ref, bf16[2048,1024]{1,0:T(8,128)(2,1)S(1)} %copy-done.2, ...), custom_call_target="tpu_custom_call" | custom-call | tf_op jit(solution)/shard_map/grad_kernel/pallas_call | solution.py:138
  398.3 5.3 %collective-permute-start.20 = (bf16[256,2048]{1,0:T(8,128)(2,1)S(1)}, bf16[256,2048]{1,0:T(8,128)(2,1)S(1)}, u32[]{:S(2)}, u32[]{:S(2)}) collective-permute-start(bf16[256,2048]{1,0:T(8,128)(2,1)S(1)} %pad_maximum_fusion), channel_id=1, source_target_pairs={{0,16},{2,18},{4,20},{6,22},{8,24},{10,26},{12,28},{14,30},{16,0},... | collective-permute-start | bytes 3145736 | tf_op jit(solution)/shard_map/ppermute | solution.py:202
  405.0 4.3 collective-permute-done.7
  416.7 5.4 %collective-permute-start.11 = (f32[128,128]{1,0:T(8,128)S(1)}, f32[128,128]{1,0:T(8,128)S(1)}, u32[]{:S(2)}, u32[]{:S(2)}) collective-permute-start(f32[128,128]{1,0:T(8,128)S(1)} %get-tuple-element.47), channel_id=1, source_target_pairs={{0,24},{2,26},{4,28},{6,30},{8,0},{10,2},{12,4},{14,6},{16,8},{18,... | collective-permute-start | bytes 196616 | tf_op jit(solution)/shard_map/ppermute | solution.py:202
  423.1 29.7 %collective-permute-done.20 = bf16[256,2048]{1,0:T(8,128)(2,1)S(1)} collective-permute-done((bf16[256,2048]{1,0:T(8,128)(2,1)S(1)}, bf16[256,2048]{1,0:T(8,128)(2,1)S(1)}, u32[]{:S(2)}, u32[]{:S(2)}) %collective-permute-start.20) | collective-permute-done | bytes 1048608 | tf_op jit(solution)/shard_map/ppermute | solution.py:202
  452.8 3.1 fusion.2
  (125 shorter events, 72.1 us)
Async XLA Ops:
  7.2 52.5 %all-gather.5.cloned.1.call-start = ((), (), s32[]{:S(2)}) async-start(), calls=%async_computation.1 | async-start | bytes 12582912 | tf_op jit(solution)/shard_map/all_gather | solution.py:271
  7.9 327.8 %all-gather.3.cloned.1.call-start = ((), (), s32[]{:S(2)}) async-start(), calls=%async_computation | async-start | bytes 17825792 | tf_op jit(solution)/shard_map/all_gather | solution.py:272
  8.7 4.9 %collective-permute-start = (bf16[128,128]{1,0:T(8,128)(2,1)S(1)}, bf16[128,128]{1,0:T(8,128)(2,1)S(1)}, u32[]{:S(2)}, u32[]{:S(2)}) collective-permute-start(bf16[128,128]{1,0:T(8,128)(2,1)S(1)} %bitcast.141), channel_id=1, source_target_pairs={{0,2},{2,0},{4,6},{6,4},{8,10},{10,8},{12,14},{14,12},{16,18},{18,... | collective-permute-start | bytes 98312 | tf_op jit(solution)/shard_map/ppermute | solution.py:196
  18.0 9.9 %collective-permute-start.2 = (bf16[2,2,128,128]{3,2,1,0:T(8,128)(2,1)S(1)}, bf16[2,2,128,128]{3,2,1,0:T(8,128)(2,1)S(1)}, u32[]{:S(2)}, u32[]{:S(2)}) collective-permute-start(bf16[2,2,128,128]{3,2,1,0:T(8,128)(2,1)S(1)} %pad_maximum_fusion.3), channel_id=1, source_target_pairs={{0,24},{2,26},{4,28},{6,30},{8,0},{10,2},{12,4},{14,6},{16,8},{18,... | collective-permute-start | bytes 393224 | tf_op jit(solution)/shard_map/ppermute | solution.py:202
  23.4 12.0 %collective-permute-start.5 = (bf16[2048,128]{1,0:T(8,128)(2,1)S(1)}, bf16[2048,128]{1,0:T(8,128)(2,1)S(1)}, u32[]{:S(2)}, u32[]{:S(2)}) collective-permute-start(bf16[2048,128]{1,0:T(8,128)(2,1)S(1)} %slice.118), channel_id=1, source_target_pairs={{0,2},{2,4},{4,6},{6,8},{8,10},{10,12},{12,14},{14,16},{16,18},{18... | collective-permute-start | bytes 1572872 | tf_op jit(solution)/shard_map/ppermute | solution.py:269
  27.0 7.5 %collective-permute-start.3 = (bf16[2,2,128,128]{3,2,1,0:T(8,128)(2,1)S(1)}, bf16[2,2,128,128]{3,2,1,0:T(8,128)(2,1)S(1)}, u32[]{:S(2)}, u32[]{:S(2)}) collective-permute-start(bf16[2,2,128,128]{3,2,1,0:T(8,128)(2,1)S(1)} %pad_maximum_fusion.3), channel_id=1, source_target_pairs={{0,16},{2,18},{4,20},{6,22},{8,24},{10,26},{12,28},{14,30},{16,0},... | collective-permute-start | bytes 393224 | tf_op jit(solution)/shard_map/ppermute | solution.py:202
  27.0 7.5 %collective-permute-start.4 = (bf16[2,2,128,128]{3,2,1,0:T(8,128)(2,1)S(1)}, bf16[2,2,128,128]{3,2,1,0:T(8,128)(2,1)S(1)}, u32[]{:S(2)}, u32[]{:S(2)}) collective-permute-start(bf16[2,2,128,128]{3,2,1,0:T(8,128)(2,1)S(1)} %pad_maximum_fusion.3), channel_id=1, source_target_pairs={{0,8},{2,10},{4,12},{6,14},{8,16},{10,18},{12,20},{14,22},{16,24},... | collective-permute-start | bytes 393224 | tf_op jit(solution)/shard_map/ppermute | solution.py:202
  68.1 42.8 %collective-permute-start.14 = (bf16[2,256,1024]{2,1,0:T(8,128)(2,1)}, bf16[2,256,1024]{2,1,0:T(8,128)(2,1)}, u32[]{:S(2)}, u32[]{:S(2)}) collective-permute-start(bf16[2,256,1024]{2,1,0:T(8,128)(2,1)} %get-tuple-element.31), channel_id=1, source_target_pairs={{0,4},{2,6},{4,0},{6,2},{8,12},{10,14},{12,8},{14,10},{16,20},{18,... | collective-permute-start | bytes 3145736 | tf_op jit(solution)/shard_map/ppermute | solution.py:199
  71.5 52.5 %collective-permute-start.12 = (bf16[2,256,1024]{2,1,0:T(8,128)(2,1)}, bf16[2,256,1024]{2,1,0:T(8,128)(2,1)}, u32[]{:S(2)}, u32[]{:S(2)}) collective-permute-start(bf16[2,256,1024]{2,1,0:T(8,128)(2,1)} %get-tuple-element.29), channel_id=1, source_target_pairs={{0,2},{2,0},{4,6},{6,4},{8,10},{10,8},{12,14},{14,12},{16,18},{18,... | collective-permute-start | bytes 3145736 | tf_op jit(solution)/shard_map/ppermute | solution.py:196
  88.2 45.2 %collective-permute-start.28 = (bf16[2,256,1024]{2,1,0:T(8,128)(2,1)}, bf16[2,256,1024]{2,1,0:T(8,128)(2,1)}, u32[]{:S(2)}, u32[]{:S(2)}) collective-permute-start(bf16[2,256,1024]{2,1,0:T(8,128)(2,1)} %get-tuple-element.43), channel_id=1, source_target_pairs={{0,4},{2,6},{4,0},{6,2},{8,12},{10,14},{12,8},{14,10},{16,20},{18,... | collective-permute-start | bytes 3145736 | tf_op jit(solution)/shard_map/ppermute | solution.py:199
  88.7 65.1 %collective-permute-start.26 = (bf16[2,256,1024]{2,1,0:T(8,128)(2,1)}, bf16[2,256,1024]{2,1,0:T(8,128)(2,1)}, u32[]{:S(2)}, u32[]{:S(2)}) collective-permute-start(bf16[2,256,1024]{2,1,0:T(8,128)(2,1)} %get-tuple-element.41), channel_id=1, source_target_pairs={{0,2},{2,0},{4,6},{6,4},{8,10},{10,8},{12,14},{14,12},{16,18},{18,... | collective-permute-start | bytes 3145736 | tf_op jit(solution)/shard_map/ppermute | solution.py:196
  96.7 59.4 %collective-permute-start.23 = (bf16[2,256,1024]{2,1,0:T(8,128)(2,1)S(1)}, bf16[2,256,1024]{2,1,0:T(8,128)(2,1)S(1)}, u32[]{:S(2)}, u32[]{:S(2)}) collective-permute-start(bf16[2,256,1024]{2,1,0:T(8,128)(2,1)S(1)} %get-tuple-element.39), channel_id=1, source_target_pairs={{0,4},{2,6},{4,0},{6,2},{8,12},{10,14},{12,8},{14,10},{16,20},{18,... | collective-permute-start | bytes 3145736 | tf_op jit(solution)/shard_map/ppermute | solution.py:199
  110.9 77.6 %collective-permute-start.21 = (bf16[2,256,1024]{2,1,0:T(8,128)(2,1)S(1)}, bf16[2,256,1024]{2,1,0:T(8,128)(2,1)S(1)}, u32[]{:S(2)}, u32[]{:S(2)}) collective-permute-start(bf16[2,256,1024]{2,1,0:T(8,128)(2,1)S(1)} %get-tuple-element.37), channel_id=1, source_target_pairs={{0,2},{2,0},{4,6},{6,4},{8,10},{10,8},{12,14},{14,12},{16,18},{18,... | collective-permute-start | bytes 3145736 | tf_op jit(solution)/shard_map/ppermute | solution.py:196
  124.0 69.8 %collective-permute-start.18 = (bf16[2,256,1024]{2,1,0:T(8,128)(2,1)S(1)}, bf16[2,256,1024]{2,1,0:T(8,128)(2,1)S(1)}, u32[]{:S(2)}, u32[]{:S(2)}) collective-permute-start(bf16[2,256,1024]{2,1,0:T(8,128)(2,1)S(1)} %get-tuple-element.35), channel_id=1, source_target_pairs={{0,4},{2,6},{4,0},{6,2},{8,12},{10,14},{12,8},{14,10},{16,20},{18,... | collective-permute-start | bytes 3145736 | tf_op jit(solution)/shard_map/ppermute | solution.py:199
  133.4 100.1 %collective-permute-start.16 = (bf16[2,256,1024]{2,1,0:T(8,128)(2,1)S(1)}, bf16[2,256,1024]{2,1,0:T(8,128)(2,1)S(1)}, u32[]{:S(2)}, u32[]{:S(2)}) collective-permute-start(bf16[2,256,1024]{2,1,0:T(8,128)(2,1)S(1)} %get-tuple-element.33), channel_id=1, source_target_pairs={{0,2},{2,0},{4,6},{6,4},{8,10},{10,8},{12,14},{14,12},{16,18},{18,... | collective-permute-start | bytes 3145736 | tf_op jit(solution)/shard_map/ppermute | solution.py:196
  153.8 244.4 %collective-permute-start.15 = (bf16[256,1024]{1,0:T(8,128)(2,1)}, bf16[256,1024]{1,0:T(8,128)(2,1)}, u32[]{:S(2)}, u32[]{:S(2)}) collective-permute-start(bf16[256,1024]{1,0:T(8,128)(2,1)} %fusion.10), channel_id=1, source_target_pairs={{0,2},{2,0},{4,6},{6,4},{8,10},{10,8},{12,14},{14,12},{16,18},{18,... | collective-permute-start | bytes 1572872 | tf_op jit(solution)/shard_map/ppermute | solution.py:196
  156.1 256.0 %collective-permute-start.13 = (bf16[256,1024]{1,0:T(8,128)(2,1)}, bf16[256,1024]{1,0:T(8,128)(2,1)}, u32[]{:S(2)}, u32[]{:S(2)}) collective-permute-start(bf16[256,1024]{1,0:T(8,128)(2,1)} %fusion.9), channel_id=1, source_target_pairs={{0,4},{2,6},{4,0},{6,2},{8,12},{10,14},{12,8},{14,10},{16,20},{18,... | collective-permute-start | bytes 1572872 | tf_op jit(solution)/shard_map/ppermute | solution.py:199
  188.5 89.9 %collective-permute-start.29 = (bf16[256,1024]{1,0:T(8,128)(2,1)S(1)}, bf16[256,1024]{1,0:T(8,128)(2,1)S(1)}, u32[]{:S(2)}, u32[]{:S(2)}) collective-permute-start(bf16[256,1024]{1,0:T(8,128)(2,1)S(1)} %fusion.16), channel_id=1, source_target_pairs={{0,2},{2,0},{4,6},{6,4},{8,10},{10,8},{12,14},{14,12},{16,18},{18,... | collective-permute-start | bytes 1572872 | tf_op jit(solution)/shard_map/ppermute | solution.py:196
  193.8 85.9 %collective-permute-start.27 = (bf16[256,1024]{1,0:T(8,128)(2,1)S(1)}, bf16[256,1024]{1,0:T(8,128)(2,1)S(1)}, u32[]{:S(2)}, u32[]{:S(2)}) collective-permute-start(bf16[256,1024]{1,0:T(8,128)(2,1)S(1)} %fusion.15), channel_id=1, source_target_pairs={{0,4},{2,6},{4,0},{6,2},{8,12},{10,14},{12,8},{14,10},{16,20},{18,... | collective-permute-start | bytes 1572872 | tf_op jit(solution)/shard_map/ppermute | solution.py:199
  233.4 58.8 %collective-permute-start.24 = (bf16[256,1024]{1,0:T(8,128)(2,1)S(1)}, bf16[256,1024]{1,0:T(8,128)(2,1)S(1)}, u32[]{:S(2)}, u32[]{:S(2)}) collective-permute-start(bf16[256,1024]{1,0:T(8,128)(2,1)S(1)} %fusion.14), channel_id=1, source_target_pairs={{0,2},{2,0},{4,6},{6,4},{8,10},{10,8},{12,14},{14,12},{16,18},{18,... | collective-permute-start | bytes 1572872 | tf_op jit(solution)/shard_map/ppermute | solution.py:196
  278.4 16.7 %collective-permute-start.22 = (bf16[256,1024]{1,0:T(8,128)(2,1)S(1)}, bf16[256,1024]{1,0:T(8,128)(2,1)S(1)}, u32[]{:S(2)}, u32[]{:S(2)}) collective-permute-start(bf16[256,1024]{1,0:T(8,128)(2,1)S(1)} %fusion.13), channel_id=1, source_target_pairs={{0,4},{2,6},{4,0},{6,2},{8,12},{10,14},{12,8},{14,10},{16,20},{18,... | collective-permute-start | bytes 1572872 | tf_op jit(solution)/shard_map/ppermute | solution.py:199
  279.7 20.9 %collective-permute-start.19 = (bf16[256,1024]{1,0:T(8,128)(2,1)S(1)}, bf16[256,1024]{1,0:T(8,128)(2,1)S(1)}, u32[]{:S(2)}, u32[]{:S(2)}) collective-permute-start(bf16[256,1024]{1,0:T(8,128)(2,1)S(1)} %fusion.12), channel_id=1, source_target_pairs={{0,2},{2,0},{4,6},{6,4},{8,10},{10,8},{12,14},{14,12},{16,18},{18,... | collective-permute-start | bytes 1572872 | tf_op jit(solution)/shard_map/ppermute | solution.py:196
  292.2 71.6 %collective-permute-start.17 = (bf16[256,1024]{1,0:T(8,128)(2,1)}, bf16[256,1024]{1,0:T(8,128)(2,1)}, u32[]{:S(2)}, u32[]{:S(2)}) collective-permute-start(bf16[256,1024]{1,0:T(8,128)(2,1)} %fusion.11), channel_id=1, source_target_pairs={{0,4},{2,6},{4,0},{6,2},{8,12},{10,14},{12,8},{14,10},{16,20},{18,... | collective-permute-start | bytes 1572872 | tf_op jit(solution)/shard_map/ppermute | solution.py:199
  295.1 127.0 %collective-permute-start.30 = (bf16[256,2048]{1,0:T(8,128)(2,1)}, bf16[256,2048]{1,0:T(8,128)(2,1)}, u32[]{:S(2)}, u32[]{:S(2)}) collective-permute-start(bf16[256,2048]{1,0:T(8,128)(2,1)} %pad_maximum_fusion.2), channel_id=1, source_target_pairs={{0,24},{2,26},{4,28},{6,30},{8,0},{10,2},{12,4},{14,6},{16,8},{18,... | collective-permute-start | bytes 3145736 | tf_op jit(solution)/shard_map/ppermute | solution.py:202
  362.1 15.3 %collective-permute-start.6 = (bf16[2048,128]{1,0:T(8,128)(2,1)S(1)}, bf16[2048,128]{1,0:T(8,128)(2,1)S(1)}, u32[]{:S(2)}, u32[]{:S(2)}) collective-permute-start(bf16[2048,128]{1,0:T(8,128)(2,1)S(1)} %slice.156), channel_id=1, source_target_pairs={{2,0},{4,2},{6,4},{8,6},{10,8},{12,10},{14,12},{16,14},{18,16},{20... | collective-permute-start | bytes 1572872 | tf_op jit(solution)/shard_map/ppermute | solution.py:282
  363.8 59.3 %collective-permute-start.25 = (bf16[256,2048]{1,0:T(8,128)(2,1)S(1)}, bf16[256,2048]{1,0:T(8,128)(2,1)S(1)}, u32[]{:S(2)}, u32[]{:S(2)}) collective-permute-start(bf16[256,2048]{1,0:T(8,128)(2,1)S(1)} %pad_maximum_fusion.1), channel_id=1, source_target_pairs={{0,8},{2,10},{4,12},{6,14},{8,16},{10,18},{12,20},{14,22},{16,24},... | collective-permute-start | bytes 3145736 | tf_op jit(solution)/shard_map/ppermute | solution.py:202
  397.0 12.3 %collective-permute-start.7 = (f32[4,2,128,128]{3,2,1,0:T(8,128)S(1)}, f32[4,2,128,128]{3,2,1,0:T(8,128)S(1)}, u32[]{:S(2)}, u32[]{:S(2)}) collective-permute-start(f32[4,2,128,128]{3,2,1,0:T(8,128)S(1)} %select_bitcast_fusion), channel_id=1, source_target_pairs={{0,2},{2,0},{4,6},{6,4},{8,10},{10,8},{12,14},{14,12},{16,18},{18,... | collective-permute-start | bytes 1572872 | tf_op jit(solution)/shard_map/ppermute | solution.py:196
  398.3 54.5 %collective-permute-start.20 = (bf16[256,2048]{1,0:T(8,128)(2,1)S(1)}, bf16[256,2048]{1,0:T(8,128)(2,1)S(1)}, u32[]{:S(2)}, u32[]{:S(2)}) collective-permute-start(bf16[256,2048]{1,0:T(8,128)(2,1)S(1)} %pad_maximum_fusion), channel_id=1, source_target_pairs={{0,16},{2,18},{4,20},{6,22},{8,24},{10,26},{12,28},{14,30},{16,0},... | collective-permute-start | bytes 3145736 | tf_op jit(solution)/shard_map/ppermute | solution.py:202
  409.4 7.3 %collective-permute-start.8 = (f32[4,128,128]{2,1,0:T(8,128)S(1)}, f32[4,128,128]{2,1,0:T(8,128)S(1)}, u32[]{:S(2)}, u32[]{:S(2)}) collective-permute-start(f32[4,128,128]{2,1,0:T(8,128)S(1)} %select_bitcast_fusion.1), channel_id=1, source_target_pairs={{0,4},{2,6},{4,0},{6,2},{8,12},{10,14},{12,8},{14,10},{16,20},{18,... | collective-permute-start | bytes 786440 | tf_op jit(solution)/shard_map/ppermute | solution.py:199
  416.7 39.1 %collective-permute-start.11 = (f32[128,128]{1,0:T(8,128)S(1)}, f32[128,128]{1,0:T(8,128)S(1)}, u32[]{:S(2)}, u32[]{:S(2)}) collective-permute-start(f32[128,128]{1,0:T(8,128)S(1)} %get-tuple-element.47), channel_id=1, source_target_pairs={{0,24},{2,26},{4,28},{6,30},{8,0},{10,2},{12,4},{14,6},{16,8},{18,... | collective-permute-start | bytes 196616 | tf_op jit(solution)/shard_map/ppermute | solution.py:202
  422.1 33.7 %collective-permute-start.10 = (f32[128,128]{1,0:T(8,128)S(1)}, f32[128,128]{1,0:T(8,128)S(1)}, u32[]{:S(2)}, u32[]{:S(2)}) collective-permute-start(f32[128,128]{1,0:T(8,128)S(1)} %get-tuple-element.48), channel_id=1, source_target_pairs={{0,16},{2,18},{4,20},{6,22},{8,24},{10,26},{12,28},{14,30},{16,0},... | collective-permute-start | bytes 196616 | tf_op jit(solution)/shard_map/ppermute | solution.py:202
  422.1 33.7 %collective-permute-start.9 = (f32[128,128]{1,0:T(8,128)S(1)}, f32[128,128]{1,0:T(8,128)S(1)}, u32[]{:S(2)}, u32[]{:S(2)}) collective-permute-start(f32[128,128]{1,0:T(8,128)S(1)} %get-tuple-element.46), channel_id=1, source_target_pairs={{0,8},{2,10},{4,12},{6,14},{8,16},{10,18},{12,20},{14,22},{16,24},... | collective-permute-start | bytes 196616 | tf_op jit(solution)/shard_map/ppermute | solution.py:202
  (20 other events, 433.6 us)
Sparse Core Ops, SparseCore 0:
  9.6 22.5 all-gather.4
  34.9 300.7 all-gather.2

commit v3 on v2

--- a/solution.py
+++ b/solution.py
@@ -185,6 +185,66 @@
     )(place, grad_full, grad_full, grad_full, grad_full, gated, gated)
 
 
+def product_kernel(slots, place_ref, grad_hbm, *refs):
+    pieces, (mixed_ref, gate_ref, gate_grad_ref, conv_grad_ref, grad, sems) = refs[: 5 * slots], refs[5 * slots :]
+    step = pl.program_id(0)
+    rows = pieces[0].shape[1]
+
+    @pl.when(step == 0)
+    def _():
+        copies = [
+            pltpu.make_async_copy(
+                grad_hbm.at[pl.ds(pl.multiple_of(place_ref[k] * rows, rows), rows)],
+                grad.at[pl.ds(k * rows, rows)],
+                sems.at[k],
+            )
+            for k in range(4 * slots)
+        ]
+        for copy in copies:
+            copy.start()
+        for copy in copies:
+            copy.wait()
+
+    upper = step < pl.num_programs(0) // 2
+    wide = []
+    for k in range(slots):
+        own, by_x, by_y, diag_a, diag_b = pieces[5 * k : 5 * k + 5]
+        wide += [own[...], by_x[...], by_y[...], jnp.where(upper, diag_a[...], diag_b[...])]
+    total = jnp.dot(jnp.concatenate(wide, axis=1), grad[...], preferred_element_type=F32)
+    gate_grad_ref[...] = total * mixed_ref[...].astype(F32)
+    conv_grad_ref[...] = (total * gate_ref[...].astype(F32)).astype(BF16)
+
+
+def run_product(place, grad_full, pieces, mixed, gate):
+    chan, seq_len = mixed.shape
+    depth = grad_full.shape[0]
+    rows = pieces[0].shape[1]
+    slots = len(pieces) // 5
+    group = min(512, chan // 2)
+    half = chan // 2 // group
+    full = lambda width: pl.BlockSpec((group, width), lambda m, place: (m, 0))
+    low = pl.BlockSpec((group, rows), lambda m, place: (jnp.minimum(m, half - 1), 0))
+    high = pl.BlockSpec((group, rows), lambda m, place: (jnp.maximum(m - half, 0), 0))
+    return pl.pallas_call(
+        lambda *refs: product_kernel(slots, *refs),
+        grid_spec=pltpu.PrefetchScalarGridSpec(
+            num_scalar_prefetch=1,
+            grid=(chan // group,),
+            in_specs=[pl.BlockSpec(memory_space=pl.ANY)]
+            + [full(rows), full(rows), full(rows), low, high] * slots
+            + [full(seq_len), full(seq_len)],
+            out_specs=[full(seq_len), full(seq_len)],
+            scratch_shapes=[pltpu.VMEM((depth, seq_len), BF16), pltpu.SemaphoreType.DMA((4 * slots,))],
+        ),
+        out_shape=[
+            jax.ShapeDtypeStruct((chan, seq_len), F32),
+            jax.ShapeDtypeStruct((chan, seq_len), BF16),
+        ],
+        compiler_params=pltpu.CompilerParams(vmem_limit_bytes=50 * MIB),
+        name="product_kernel",
+    )(place, grad_full, *pieces, mixed, gate)
+
+
 class Layout:
     def __init__(self):
         self.count = lax.axis_size("ctx")
@@ -229,6 +289,23 @@
     for by in range(1, at.depth):
         total = total + at.shift_z(at_z(by), by)
     return total
+
+
+def gather_weight(at, own):
+    half = own.shape[0] // 2
+    pieces, place = [], []
+    before = None
+    for by in sorted(range(at.depth), key=lambda d: min(d, at.depth - d)):
+        if by == 0:
+            slot = own
+        else:
+            source = own if before is None else lax.optimization_barrier((own, before))[0]
+            slot = before = at.shift_z(source, by)
+        from_x, from_y = at.swap_x(slot), at.swap_y(slot)
+        pieces += [slot, from_x, from_y, at.swap_x(from_y[:half]), at.swap_y(from_x[half:])]
+        base = 4 * ((at.z - by) % at.depth)
+        place += [base + 2 * (at.y ^ dy) + (at.x ^ dx) for dy in range(2) for dx in range(2)]
+    return pieces, jnp.stack(place).astype(jnp.int32)
 
 
 def reduce_weight(at, grad_full, gated, rows):
@@ -269,16 +346,12 @@
     prior = lax.ppermute(kv_product[:, seq_len - taps :], "ctx", to_right)
     all_filters = gather_filters(at, filters.reshape(chan_count, taps))
     grad_full = lax.all_gather(out_grad, "fsdp", axis=0, tiled=True)
-    w_full = lax.all_gather(w_out, "ctx", axis=0, tiled=True)
+    pieces, place = gather_weight(at, w_out.T)
 
     mixed, gated = run_mix(all_filters, kv_product, prior, gate_values, forward, backward)
     w_grad = reduce_weight(at, grad_full, gated, w_out.shape[0]) * norm_scale
 
-    mix_grad = lax.dot_general(
-        w_full, grad_full, (((0,), (0,)), ((), ())), preferred_element_type=F32
-    )
-    conv_grad = (mix_grad * gate_values.astype(F32)).astype(BF16)
-    gate_grad = mix_grad * mixed.astype(F32)
+    gate_grad, conv_grad = run_product(place, grad_full, pieces, mixed, gate_values)
     after = lax.ppermute(conv_grad[:, :taps], "ctx", to_left)
     kv_grad, filt_part = run_grad(all_filters, conv_grad, after, kv_product, forward, backward)
     filter_grad = reduce_filters(at, filt_part, chan_count) * norm_scale

time: 464 us -> 537 us (1.16); the launches traced: 463 us -> 527 us
  waiting for transfers between devices: 246 us -> 304 us
  Pallas kernels: 68.1 us -> 96.2 us
  matrix products: 21.5 us -> 0 us
  local copies, waits for them, and re-layouts: 11.9 us -> 28.5 us
  starting transfers between devices: 73.2 us -> 60.4 us
    ppermute x9 -> x12, waiting for transfers between devices: 36.2 us -> 135 us  [shift_z(): lax.ppermute(array, 'ctx', [(i, (i + 4 * by) % self.count) for i in range...]
    ppermute x10 -> x18, waiting for transfers between devices: 20.2 us -> 73.1 us  [swap_y(): return lax.ppermute(array, 'ctx', [(i, i ^ 2) for i in range(self.count)])]
    ppermute x10 -> x18, waiting for transfers between devices: 145 us -> 95.2 us  [swap_x(): return lax.ppermute(array, 'ctx', [(i, i ^ 1) for i in range(self.count)])]
    all_gather x1 -> x0, waiting for transfers between devices: 34.8 us -> none  [on_device(): w_full = lax.all_gather(w_out, 'ctx', axis=0, tiled=True)]
    pallas_call x0 -> x1, Pallas kernels: none -> 27.8 us  [run_product(): pl.pallas_call(lambda *refs: product_kernel(slots, *refs), grid_spec=pltp...]
    dot_general x1 -> x0, matrix products: 21.5 us -> none  [on_device(): lax.dot_general(w_full, grad_full, (((0,), (0,)), ((), ())), preferred_el...]
    slice x0 -> x8, local copies, waits for them, and re-layouts: none -> 10.9 us  [the longest x4 5.81 us: gather_weight(): from_x[half:]]
    ppermute x1, waiting for transfers between devices: 8.48 us -> 0.01 us  [on_device(): after = lax.ppermute(conv_grad[:, :taps], 'ctx', to_left)]
  transfers between devices with their start and end apart: 33 -> 51, of which waited for: 19 -> 22; matrix products, arithmetic and copies ran while one was open for 11% -> 7% of each run, Pallas kernels for 15% -> 18%
where the time goes in v3:
time: 537 us; the launch traced here: 527 us
  waiting for transfers between devices  304 us (57%)
  Pallas kernels  96.2 us (18%)
  starting transfers between devices  60.4 us (11%)
  local copies, waits for them, and re-layouts  28.5 us (5%)
  other arithmetic  23.3 us (4%)
  between operations  14.7 us (3%)
    ppermute x12, waiting for transfers between devices, shift_z(): lax.ppermute(array, 'ctx', [(i, (i + 4 * by) % self.count) for i in range...  135 us
    ppermute x18, waiting for transfers between devices, swap_x(): return lax.ppermute(array, 'ctx', [(i, i ^ 1) for i in range(self.count)])  95.2 us
    ppermute x18, waiting for transfers between devices, swap_y(): return lax.ppermute(array, 'ctx', [(i, i ^ 2) for i in range(self.count)])  73.1 us
    pallas_call x4, Pallas kernels, run_weight(): pl.pallas_call(weight_kernel, grid_spec=pltpu.PrefetchScalarGridSpec(num_...  32.8 us
    pallas_call x1, Pallas kernels, run_product(): pl.pallas_call(lambda *refs: product_kernel(slots, *refs), grid_spec=pltp...  27.8 us
    ppermute x18, starting transfers between devices, swap_x(): return lax.ppermute(array, 'ctx', [(i, i ^ 1) for i in range(self.count)])  23.5 us
    pallas_call x1, Pallas kernels, run_grad(): pl.pallas_call(grad_kernel, grid=(chan // group,), in_specs=[rows(taps),...  19.6 us
    ppermute x12, starting transfers between devices, shift_z(): lax.ppermute(array, 'ctx', [(i, (i + 4 * by) % self.count) for i in range...  17.6 us
  transfers between devices with their start and end apart: 51, of which 22 were waited for; matrix products, arithmetic and copies ran while one was open for 7% of the time, Pallas kernels for 18%

profile of v3, /device:TPU:0, one launch (start us, length us, event | category | flops | bytes accessed | tf_op | source)
XLA Modules:
  0.0 527.5 jit_solution(14851087382458282303)
XLA Ops:
  8.9 3.1 collective-permute-start.4
  12.0 25.3 %collective-permute-done.4.refs_7_ = bf16[2048,256]{1,0:T(8,128)(2,1)} collective-permute-done((bf16[2048,256]{1,0:T(8,128)(2,1)S(1)}, bf16[2048,256]{1,0:T(8,128)(2,1)}, u32[]{:S(2)}, u32[]{:S(2)}) %collective-permute-start.4) | collective-permute-done | bytes 1048608 | tf_op jit(solution)/shard_map/ppermute | solution.py:262
  42.6 19.2 %collective-permute-done.9.refs_12_ = bf16[2048,256]{1,0:T(8,128)(2,1)} collective-permute-done((bf16[2048,256]{1,0:T(8,128)(2,1)S(1)}, bf16[2048,256]{1,0:T(8,128)(2,1)}, u32[]{:S(2)}, u32[]{:S(2)}) %collective-permute-start.9) | collective-permute-done | bytes 1048608 | tf_op jit(solution)/shard_map/ppermute | solution.py:262
  64.3 23.5 %collective-permute-done.20 = bf16[2,128,128]{2,1,0:T(8,128)(2,1)S(1)} collective-permute-done((bf16[2,128,128]{2,1,0:T(8,128)(2,1)S(1)}, bf16[2,128,128]{2,1,0:T(8,128)(2,1)S(1)}, u32[]{:S(2)}, u32[]{:S(2)}) %collective-permute-start.20) | collective-permute-done | bytes 65568 | tf_op jit(solution)/shard_map/ppermute | solution.py:259
  89.9 21.5 %collective-permute-done.21 = bf16[2,2,128,128]{3,2,1,0:T(8,128)(2,1)S(1)} collective-permute-done((bf16[2,2,128,128]{3,2,1,0:T(8,128)(2,1)S(1)}, bf16[2,2,128,128]{3,2,1,0:T(8,128)(2,1)S(1)}, u32[]{:S(2)}, u32[]{:S(2)}) %collective-permute-start.21) | collective-permute-done | bytes 131104 | tf_op jit(solution)/shard_map/ppermute | solution.py:262
  112.0 8.2 %collective-permute-done.22 = bf16[2,2,128,128]{3,2,1,0:T(8,128)(2,1)S(1)} collective-permute-done((bf16[2,2,128,128]{3,2,1,0:T(8,128)(2,1)S(1)}, bf16[2,2,128,128]{3,2,1,0:T(8,128)(2,1)S(1)}, u32[]{:S(2)}, u32[]{:S(2)}) %collective-permute-start.22) | collective-permute-done | bytes 131104 | tf_op jit(solution)/shard_map/ppermute | solution.py:262
  120.2 7.2 %collective-permute-done.23 = bf16[2,2,128,128]{3,2,1,0:T(8,128)(2,1)S(1)} collective-permute-done((bf16[2,2,128,128]{3,2,1,0:T(8,128)(2,1)S(1)}, bf16[2,2,128,128]{3,2,1,0:T(8,128)(2,1)S(1)}, u32[]{:S(2)}, u32[]{:S(2)}) %collective-permute-start.23) | collective-permute-done | bytes 131104 | tf_op jit(solution)/shard_map/ppermute | solution.py:262
  136.1 17.7 %collective-permute-done.5.refs_8_ = bf16[2048,256]{1,0:T(8,128)(2,1)} collective-permute-done((bf16[2048,256]{1,0:T(8,128)(2,1)}, bf16[2048,256]{1,0:T(8,128)(2,1)}, u32[]{:S(2)}, u32[]{:S(2)}) %collective-permute-start.5) | collective-permute-done | bytes 1048608 | tf_op jit(solution)/shard_map/ppermute | solution.py:256
  153.8 2.2 collective-permute-start.24
  157.6 18.7 %collective-permute-done.10.refs_13_ = bf16[2048,256]{1,0:T(8,128)(2,1)} collective-permute-done((bf16[2048,256]{1,0:T(8,128)(2,1)}, bf16[2048,256]{1,0:T(8,128)(2,1)}, u32[]{:S(2)}, u32[]{:S(2)}) %collective-permute-start.10) | collective-permute-done | bytes 1048608 | tf_op jit(solution)/shard_map/ppermute | solution.py:256
  180.0 18.8 %collective-permute-done.15.refs_18_ = bf16[2048,256]{1,0:T(8,128)(2,1)} collective-permute-done((bf16[2048,256]{1,0:T(8,128)(2,1)}, bf16[2048,256]{1,0:T(8,128)(2,1)}, u32[]{:S(2)}, u32[]{:S(2)}) %collective-permute-start.15) | collective-permute-done | bytes 1048608 | tf_op jit(solution)/shard_map/ppermute | solution.py:256
  207.7 2.5 collective-permute-start.12
  210.2 11.0 %collective-permute-done.2.refs_5_ = bf16[1024,256]{1,0:T(8,128)(2,1)S(1)} collective-permute-done((bf16[1024,256]{1,0:T(8,128)(2,1)S(1)}, bf16[1024,256]{1,0:T(8,128)(2,1)S(1)}, u32[]{:S(2)}, u32[]{:S(2)}) %collective-permute-start.2) | collective-permute-done | bytes 524320 | tf_op jit(solution)/shard_map/ppermute | solution.py:256
  222.9 9.5 %collective-permute-done.7.refs_10_ = bf16[1024,256]{1,0:T(8,128)(2,1)S(1)} collective-permute-done((bf16[1024,256]{1,0:T(8,128)(2,1)S(1)}, bf16[1024,256]{1,0:T(8,128)(2,1)S(1)}, u32[]{:S(2)}, u32[]{:S(2)}) %collective-permute-start.7) | collective-permute-done | bytes 524320 | tf_op jit(solution)/shard_map/ppermute | solution.py:256
  233.5 15.9 %mix_kernel.1 = (bf16[2048,1024]{1,0:T(8,128)(2,1)S(1)}, bf16[2048,1024]{1,0:T(8,128)(2,1)S(1)}) custom-call(bf16[2048,128]{1,0:T(8,128)(2,1)S(1)} %bitcast.148, bf16[2048,1024]{1,0:T(8,128)(2,1)S(1)} %copy-done.1, bf16[2048,128]{1,0:T(8,128)(2,1)S(1)} %collective-permute-done.24.prior_ref, bf16[2048,1024]{1,0:T(8,128)(2,1)S(1)} %copy-done.3, ...), custom_call_target="tpu_custom_call" | custom-call | tf_op jit(solution)/shard_map/mix_kernel/pallas_call | solution.py:93
  253.5 8.4 %weight_kernel.5 = (bf16[2,256,1024]{2,1,0:T(8,128)(2,1)}, bf16[2,256,1024]{2,1,0:T(8,128)(2,1)S(1)}, bf16[2,256,1024]{2,1,0:T(8,128)(2,1)}, bf16[2,256,1024]{2,1,0:T(8,128)(2,1)S(1)}) custom-call(s32[4]{0:T(128)S(1)} %get-tuple-element.60.place_ref, bf16[4096,1024]{1,0:T(8,128)(2,1)} %all-gather.2.cloned.1.call-done.refs_1_.g00.g01.g10.g11, ...), custom_call_target="tpu_custom_call" | custom-call | tf_op jit(solution)/shard_map/weight_kernel/pallas_call | solution.py:174
  266.2 27.8 %product_kernel.1 = (f32[2048,1024]{1,0:T(8,128)}, bf16[2048,1024]{1,0:T(8,128)(2,1)}) custom-call(s32[16]{0:T(128)S(1)} %stack.156.refs_0_, bf16[4096,1024]{1,0:T(8,128)(2,1)} %all-gather.2.cloned.1.call-done.refs_1_.g00.g01.g10.g11, bf16[2048,256]{1,0:T(8,128)(2,1)} %bitcast.157, bf16[2048,256]{1,0:T(8,128)(2,1)} %copy-done.21, ...), custom_call_target="tpu_custom_call" | custom-call | tf_op jit(solution)/shard_map/product_kernel/pallas_call | solution.py:228
  297.6 8.4 %weight_kernel.6 = (bf16[2,256,1024]{2,1,0:T(8,128)(2,1)}, bf16[2,256,1024]{2,1,0:T(8,128)(2,1)S(1)}, bf16[2,256,1024]{2,1,0:T(8,128)(2,1)}, bf16[2,256,1024]{2,1,0:T(8,128)(2,1)S(1)}) custom-call(s32[4]{0:T(128)S(1)} %get-tuple-element.61.place_ref, bf16[4096,1024]{1,0:T(8,128)(2,1)} %all-gather.2.cloned.1.call-done.refs_1_.g00.g01.g10.g11, ...), custom_call_target="tpu_custom_call" | custom-call | tf_op jit(solution)/shard_map/weight_kernel/pallas_call | solution.py:174
  307.9 2.6 collective-permute-start.40
  312.1 7.8 %weight_kernel.7 = (bf16[2,256,1024]{2,1,0:T(8,128)(2,1)S(1)}, bf16[2,256,1024]{2,1,0:T(8,128)(2,1)S(1)}, bf16[2,256,1024]{2,1,0:T(8,128)(2,1)S(1)}, bf16[2,256,1024]{2,1,0:T(8,128)(2,1)S(1)}) custom-call(s32[4]{0:T(128)S(1)} %get-tuple-element.62.place_ref, bf16[4096,1024]{1,0:T(8,128)(2,1)} %all-gather.2.cloned.1.call-done.refs_1_.g00.g01.g10.g11, ...), custom_call_target="tpu_custom_call" | custom-call | tf_op jit(solution)/shard_map/weight_kernel/pallas_call | solution.py:174
  321.9 8.1 %weight_kernel.4 = (bf16[2,256,1024]{2,1,0:T(8,128)(2,1)S(1)}, bf16[2,256,1024]{2,1,0:T(8,128)(2,1)S(1)}, bf16[2,256,1024]{2,1,0:T(8,128)(2,1)S(1)}, bf16[2,256,1024]{2,1,0:T(8,128)(2,1)S(1)}) custom-call(s32[4]{0:T(128)S(1)} %get-tuple-element.59.place_ref, bf16[4096,1024]{1,0:T(8,128)(2,1)} %all-gather.2.cloned.1.call-done.refs_1_.g00.g01.g10.g11, ...), custom_call_target="tpu_custom_call" | custom-call | tf_op jit(solution)/shard_map/weight_kernel/pallas_call | solution.py:174
  331.9 19.6 %grad_kernel.1 = (bf16[2048,1024]{1,0:T(8,128)(2,1)}, f32[2048,128]{1,0:T(8,128)S(1)}) custom-call(bf16[2048,128]{1,0:T(8,128)(2,1)S(1)} %bitcast.149, bf16[2048,1024]{1,0:T(8,128)(2,1)S(1)} %copy-done.4, bf16[2048,128]{1,0:T(8,128)(2,1)S(1)} %collective-permute-done.25.after_ref, bf16[2048,1024]{1,0:T(8,128)(2,1)S(1)} %copy-done.2, ...), custom_call_target="tpu_custom_call" | custom-call | tf_op jit(solution)/shard_map/grad_kernel/pallas_call | solution.py:138
  361.4 16.4 %collective-permute-done.47 = bf16[2,256,1024]{2,1,0:T(8,128)(2,1)S(1)} collective-permute-done((bf16[2,256,1024]{2,1,0:T(8,128)(2,1)S(1)}, bf16[2,256,1024]{2,1,0:T(8,128)(2,1)S(1)}, u32[]{:S(2)}, u32[]{:S(2)}) %collective-permute-start.47) | collective-permute-done | bytes 1048608 | tf_op jit(solution)/shard_map/ppermute | solution.py:259
  378.3 12.2 %collective-permute-done.26 = f32[4,2,128,128]{3,2,1,0:T(8,128)S(1)} collective-permute-done((f32[4,2,128,128]{3,2,1,0:T(8,128)S(1)}, f32[4,2,128,128]{3,2,1,0:T(8,128)S(1)}, u32[]{:S(2)}, u32[]{:S(2)}) %collective-permute-start.26) | collective-permute-done | bytes 524320 | tf_op jit(solution)/shard_map/ppermute | solution.py:256
  393.0 32.4 %collective-permute-done.27 = f32[4,128,128]{2,1,0:T(8,128)S(1)} collective-permute-done((f32[4,128,128]{2,1,0:T(8,128)S(1)}, f32[4,128,128]{2,1,0:T(8,128)S(1)}, u32[]{:S(2)}, u32[]{:S(2)}) %collective-permute-start.27) | collective-permute-done | bytes 262176 | tf_op jit(solution)/shard_map/ppermute | solution.py:259
  442.9 2.5 collective-permute-start.39
  445.4 6.4 %collective-permute-start.44 = (bf16[256,2048]{1,0:T(8,128)(2,1)}, bf16[256,2048]{1,0:T(8,128)(2,1)}, u32[]{:S(2)}, u32[]{:S(2)}) collective-permute-start(bf16[256,2048]{1,0:T(8,128)(2,1)} %pad_maximum_fusion.1), channel_id=1, source_target_pairs={{0,8},{2,10},{4,12},{6,14},{8,16},{10,18},{12,20},{14,22},{16,24},... | collective-permute-start | bytes 3145736 | tf_op jit(solution)/shard_map/ppermute | solution.py:262
  451.8 23.4 %collective-permute-done.29 = f32[128,128]{1,0:T(8,128)S(1)} collective-permute-done((f32[128,128]{1,0:T(8,128)S(1)}, f32[128,128]{1,0:T(8,128)S(1)}, u32[]{:S(2)}, u32[]{:S(2)}) %collective-permute-start.29) | collective-permute-done | bytes 65568 | tf_op jit(solution)/shard_map/ppermute | solution.py:262
  480.4 5.4 %collective-permute-done.34 = bf16[256,1024]{1,0:T(8,128)(2,1)} collective-permute-done((bf16[256,1024]{1,0:T(8,128)(2,1)}, bf16[256,1024]{1,0:T(8,128)(2,1)}, u32[]{:S(2)}, u32[]{:S(2)}) %collective-permute-start.34) | collective-permute-done | bytes 524320 | tf_op jit(solution)/shard_map/ppermute | solution.py:256
  487.1 21.1 %collective-permute-done.39 = bf16[256,2048]{1,0:T(8,128)(2,1)} collective-permute-done((bf16[256,2048]{1,0:T(8,128)(2,1)}, bf16[256,2048]{1,0:T(8,128)(2,1)}, u32[]{:S(2)}, u32[]{:S(2)}) %collective-permute-start.39) | collective-permute-done | bytes 1048608 | tf_op jit(solution)/shard_map/ppermute | solution.py:262
  508.1 8.7 %collective-permute-done.49 = bf16[256,2048]{1,0:T(8,128)(2,1)} collective-permute-done((bf16[256,2048]{1,0:T(8,128)(2,1)}, bf16[256,2048]{1,0:T(8,128)(2,1)}, u32[]{:S(2)}, u32[]{:S(2)}) %collective-permute-start.49) | collective-permute-done | bytes 1048608 | tf_op jit(solution)/shard_map/ppermute | solution.py:262
  516.9 3.8 fusion.2
  (193 shorter events, 93.4 us)
Async XLA Ops:
  7.2 246.3 %all-gather.2.cloned.1.call-start = ((), (), s32[]{:S(2)}) async-start(), calls=%async_computation | async-start | bytes 12582912 | tf_op jit(solution)/shard_map/all_gather | solution.py:348
  40.5 87.2 %collective-permute-start.1 = (bf16[2048,256]{1,0:T(8,128)(2,1)S(1)}, bf16[2048,256]{1,0:T(8,128)(2,1)S(1)}, u32[]{:S(2)}, u32[]{:S(2)}) collective-permute-start(bf16[2048,256]{1,0:T(8,128)(2,1)S(1)} %bitcast.154), channel_id=1, source_target_pairs={{0,4},{2,6},{4,0},{6,2},{8,12},{10,14},{12,8},{14,10},{16,20},{18,... | collective-permute-start | bytes 3145736 | tf_op jit(solution)/shard_map/ppermute | solution.py:259
  42.0 87.2 %collective-permute-start = (bf16[2048,256]{1,0:T(8,128)(2,1)S(1)}, bf16[2048,256]{1,0:T(8,128)(2,1)S(1)}, u32[]{:S(2)}, u32[]{:S(2)}) collective-permute-start(bf16[2048,256]{1,0:T(8,128)(2,1)S(1)} %bitcast.155), channel_id=1, source_target_pairs={{0,2},{2,0},{4,6},{6,4},{8,10},{10,8},{12,14},{14,12},{16,18},{18,... | collective-permute-start | bytes 3145736 | tf_op jit(solution)/shard_map/ppermute | solution.py:256
  61.7 68.0 %collective-permute-start.14 = (bf16[2048,256]{1,0:T(8,128)(2,1)S(1)}, bf16[2048,256]{1,0:T(8,128)(2,1)}, u32[]{:S(2)}, u32[]{:S(2)}) collective-permute-start(bf16[2048,256]{1,0:T(8,128)(2,1)S(1)} %bitcast.156), channel_id=1, source_target_pairs={{0,16},{2,18},{4,20},{6,22},{8,24},{10,26},{12,28},{14,30},{16,0},... | collective-permute-start | bytes 3145736 | tf_op jit(solution)/shard_map/ppermute | solution.py:262
  62.2 69.3 %collective-permute-start.6 = (bf16[2048,256]{1,0:T(8,128)(2,1)}, bf16[2048,256]{1,0:T(8,128)(2,1)}, u32[]{:S(2)}, u32[]{:S(2)}) collective-permute-start(bf16[2048,256]{1,0:T(8,128)(2,1)} %collective-permute-done.4.refs_7_), channel_id=1, source_target_pairs={{0,4},{2,6},{4,0},{6,2},{8,12},{10,14},{12,8},{14,10},{16,20},{18,... | collective-permute-start | bytes 3145736 | tf_op jit(solution)/shard_map/ppermute | solution.py:259
  129.2 47.1 %collective-permute-start.10 = (bf16[2048,256]{1,0:T(8,128)(2,1)}, bf16[2048,256]{1,0:T(8,128)(2,1)}, u32[]{:S(2)}, u32[]{:S(2)}) collective-permute-start(bf16[2048,256]{1,0:T(8,128)(2,1)} %collective-permute-done.9.refs_12_), channel_id=1, source_target_pairs={{0,2},{2,0},{4,6},{6,4},{8,10},{10,8},{12,14},{14,12},{16,18},{18,... | collective-permute-start | bytes 3145736 | tf_op jit(solution)/shard_map/ppermute | solution.py:256
  129.8 46.8 %collective-permute-start.16 = (bf16[2048,256]{1,0:T(8,128)(2,1)}, bf16[2048,256]{1,0:T(8,128)(2,1)}, u32[]{:S(2)}, u32[]{:S(2)}) collective-permute-start(bf16[2048,256]{1,0:T(8,128)(2,1)} %collective-permute-done.14.refs_17_), channel_id=1, source_target_pairs={{0,4},{2,6},{4,0},{6,2},{8,12},{10,14},{12,8},{14,10},{16,20},{18,... | collective-permute-start | bytes 3145736 | tf_op jit(solution)/shard_map/ppermute | solution.py:259
  131.5 67.3 %collective-permute-start.15 = (bf16[2048,256]{1,0:T(8,128)(2,1)}, bf16[2048,256]{1,0:T(8,128)(2,1)}, u32[]{:S(2)}, u32[]{:S(2)}) collective-permute-start(bf16[2048,256]{1,0:T(8,128)(2,1)} %collective-permute-done.14.refs_17_), channel_id=1, source_target_pairs={{0,2},{2,0},{4,6},{6,4},{8,10},{10,8},{12,14},{14,12},{16,18},{18,... | collective-permute-start | bytes 3145736 | tf_op jit(solution)/shard_map/ppermute | solution.py:256
  153.8 53.9 %collective-permute-start.24 = (bf16[2048,128]{1,0:T(8,128)(2,1)S(1)}, bf16[2048,128]{1,0:T(8,128)(2,1)S(1)}, u32[]{:S(2)}, u32[]{:S(2)}) collective-permute-start(bf16[2048,128]{1,0:T(8,128)(2,1)S(1)} %copy-done.26), channel_id=1, source_target_pairs={{0,2},{2,4},{4,6},{6,8},{8,10},{10,12},{12,14},{14,16},{16,18},{18... | collective-permute-start | bytes 1572872 | tf_op jit(solution)/shard_map/ppermute | solution.py:346
  156.0 65.1 %collective-permute-start.2 = (bf16[1024,256]{1,0:T(8,128)(2,1)S(1)}, bf16[1024,256]{1,0:T(8,128)(2,1)S(1)}, u32[]{:S(2)}, u32[]{:S(2)}) collective-permute-start(bf16[1024,256]{1,0:T(8,128)(2,1)S(1)} %slice.188), channel_id=1, source_target_pairs={{0,2},{2,0},{4,6},{6,4},{8,10},{10,8},{12,14},{14,12},{16,18},{18,... | collective-permute-start | bytes 1572872 | tf_op jit(solution)/shard_map/ppermute | solution.py:256
  176.3 44.9 %collective-permute-start.3 = (bf16[1024,256]{1,0:T(8,128)(2,1)S(1)}, bf16[1024,256]{1,0:T(8,128)(2,1)S(1)}, u32[]{:S(2)}, u32[]{:S(2)}) collective-permute-start(bf16[1024,256]{1,0:T(8,128)(2,1)S(1)} %slice.189), channel_id=1, source_target_pairs={{0,4},{2,6},{4,0},{6,2},{8,12},{10,14},{12,8},{14,10},{16,20},{18,... | collective-permute-start | bytes 1572872 | tf_op jit(solution)/shard_map/ppermute | solution.py:259
  176.6 55.8 %collective-permute-start.7 = (bf16[1024,256]{1,0:T(8,128)(2,1)S(1)}, bf16[1024,256]{1,0:T(8,128)(2,1)S(1)}, u32[]{:S(2)}, u32[]{:S(2)}) collective-permute-start(bf16[1024,256]{1,0:T(8,128)(2,1)S(1)} %slice.190), channel_id=1, source_target_pairs={{0,2},{2,0},{4,6},{6,4},{8,10},{10,8},{12,14},{14,12},{16,18},{18,... | collective-permute-start | bytes 1572872 | tf_op jit(solution)/shard_map/ppermute | solution.py:256
  198.8 65.1 %collective-permute-start.8 = (bf16[1024,256]{1,0:T(8,128)(2,1)}, bf16[1024,256]{1,0:T(8,128)(2,1)S(1)}, u32[]{:S(2)}, u32[]{:S(2)}) collective-permute-start(bf16[1024,256]{1,0:T(8,128)(2,1)} %slice.191), channel_id=1, source_target_pairs={{0,4},{2,6},{4,0},{6,2},{8,12},{10,14},{12,8},{14,10},{16,20},{18,... | collective-permute-start | bytes 1572872 | tf_op jit(solution)/shard_map/ppermute | solution.py:259
  207.7 57.9 %collective-permute-start.12 = (bf16[1024,256]{1,0:T(8,128)(2,1)}, bf16[1024,256]{1,0:T(8,128)(2,1)S(1)}, u32[]{:S(2)}, u32[]{:S(2)}) collective-permute-start(bf16[1024,256]{1,0:T(8,128)(2,1)} %slice.192), channel_id=1, source_target_pairs={{0,2},{2,0},{4,6},{6,4},{8,10},{10,8},{12,14},{14,12},{16,18},{18,... | collective-permute-start | bytes 1572872 | tf_op jit(solution)/shard_map/ppermute | solution.py:256
  221.2 45.0 %collective-permute-start.13 = (bf16[1024,256]{1,0:T(8,128)(2,1)}, bf16[1024,256]{1,0:T(8,128)(2,1)}, u32[]{:S(2)}, u32[]{:S(2)}) collective-permute-start(bf16[1024,256]{1,0:T(8,128)(2,1)} %slice.193), channel_id=1, source_target_pairs={{0,4},{2,6},{4,0},{6,2},{8,12},{10,14},{12,8},{14,10},{16,20},{18,... | collective-permute-start | bytes 1572872 | tf_op jit(solution)/shard_map/ppermute | solution.py:259
  221.2 45.0 %collective-permute-start.17 = (bf16[1024,256]{1,0:T(8,128)(2,1)}, bf16[1024,256]{1,0:T(8,128)(2,1)}, u32[]{:S(2)}, u32[]{:S(2)}) collective-permute-start(bf16[1024,256]{1,0:T(8,128)(2,1)} %slice.194), channel_id=1, source_target_pairs={{0,2},{2,0},{4,6},{6,4},{8,10},{10,8},{12,14},{14,12},{16,18},{18,... | collective-permute-start | bytes 1572872 | tf_op jit(solution)/shard_map/ppermute | solution.py:256
  263.9 87.7 %collective-permute-start.35 = (bf16[2,256,1024]{2,1,0:T(8,128)(2,1)}, bf16[2,256,1024]{2,1,0:T(8,128)(2,1)}, u32[]{:S(2)}, u32[]{:S(2)}) collective-permute-start(bf16[2,256,1024]{2,1,0:T(8,128)(2,1)} %get-tuple-element.41), channel_id=1, source_target_pairs={{0,2},{2,0},{4,6},{6,4},{8,10},{10,8},{12,14},{14,12},{16,18},{18,... | collective-permute-start | bytes 3145736 | tf_op jit(solution)/shard_map/ppermute | solution.py:256
  265.6 87.5 %collective-permute-start.37 = (bf16[2,256,1024]{2,1,0:T(8,128)(2,1)}, bf16[2,256,1024]{2,1,0:T(8,128)(2,1)}, u32[]{:S(2)}, u32[]{:S(2)}) collective-permute-start(bf16[2,256,1024]{2,1,0:T(8,128)(2,1)} %get-tuple-element.43), channel_id=1, source_target_pairs={{0,4},{2,6},{4,0},{6,2},{8,12},{10,14},{12,8},{14,10},{16,20},{18,... | collective-permute-start | bytes 3145736 | tf_op jit(solution)/shard_map/ppermute | solution.py:259
  296.0 34.1 %collective-permute-start.25 = (bf16[2048,128]{1,0:T(8,128)(2,1)}, bf16[2048,128]{1,0:T(8,128)(2,1)S(1)}, u32[]{:S(2)}, u32[]{:S(2)}) collective-permute-start(bf16[2048,128]{1,0:T(8,128)(2,1)} %slice.151), channel_id=1, source_target_pairs={{2,0},{4,2},{6,4},{8,6},{10,8},{12,10},{14,12},{16,14},{18,16},{20... | collective-permute-start | bytes 1572872 | tf_op jit(solution)/shard_map/ppermute | solution.py:355
  307.9 47.2 %collective-permute-start.40 = (bf16[2,256,1024]{2,1,0:T(8,128)(2,1)}, bf16[2,256,1024]{2,1,0:T(8,128)(2,1)}, u32[]{:S(2)}, u32[]{:S(2)}) collective-permute-start(bf16[2,256,1024]{2,1,0:T(8,128)(2,1)} %get-tuple-element.45), channel_id=1, source_target_pairs={{0,2},{2,0},{4,6},{6,4},{8,10},{10,8},{12,14},{14,12},{16,18},{18,... | collective-permute-start | bytes 3145736 | tf_op jit(solution)/shard_map/ppermute | solution.py:256
  310.6 47.4 %collective-permute-start.42 = (bf16[2,256,1024]{2,1,0:T(8,128)(2,1)}, bf16[2,256,1024]{2,1,0:T(8,128)(2,1)}, u32[]{:S(2)}, u32[]{:S(2)}) collective-permute-start(bf16[2,256,1024]{2,1,0:T(8,128)(2,1)} %get-tuple-element.47), channel_id=1, source_target_pairs={{0,4},{2,6},{4,0},{6,2},{8,12},{10,14},{12,8},{14,10},{16,20},{18,... | collective-permute-start | bytes 3145736 | tf_op jit(solution)/shard_map/ppermute | solution.py:259
  353.1 39.5 %collective-permute-start.31 = (bf16[2,256,1024]{2,1,0:T(8,128)(2,1)S(1)}, bf16[2,256,1024]{2,1,0:T(8,128)(2,1)S(1)}, u32[]{:S(2)}, u32[]{:S(2)}) collective-permute-start(bf16[2,256,1024]{2,1,0:T(8,128)(2,1)S(1)} %get-tuple-element.37), channel_id=1, source_target_pairs={{0,2},{2,0},{4,6},{6,4},{8,10},{10,8},{12,14},{14,12},{16,18},{18,... | collective-permute-start | bytes 3145736 | tf_op jit(solution)/shard_map/ppermute | solution.py:256
  355.1 87.7 %collective-permute-start.33 = (bf16[2,256,1024]{2,1,0:T(8,128)(2,1)S(1)}, bf16[2,256,1024]{2,1,0:T(8,128)(2,1)S(1)}, u32[]{:S(2)}, u32[]{:S(2)}) collective-permute-start(bf16[2,256,1024]{2,1,0:T(8,128)(2,1)S(1)} %get-tuple-element.39), channel_id=1, source_target_pairs={{0,4},{2,6},{4,0},{6,2},{8,12},{10,14},{12,8},{14,10},{16,20},{18,... | collective-permute-start | bytes 3145736 | tf_op jit(solution)/shard_map/ppermute | solution.py:259
  361.0 64.4 %collective-permute-start.36 = (bf16[256,1024]{1,0:T(8,128)(2,1)S(1)}, bf16[256,1024]{1,0:T(8,128)(2,1)S(1)}, u32[]{:S(2)}, u32[]{:S(2)}) collective-permute-start(bf16[256,1024]{1,0:T(8,128)(2,1)S(1)} %fusion.11), channel_id=1, source_target_pairs={{0,4},{2,6},{4,0},{6,2},{8,12},{10,14},{12,8},{14,10},{16,20},{18,... | collective-permute-start | bytes 1572872 | tf_op jit(solution)/shard_map/ppermute | solution.py:259
  377.8 49.0 %collective-permute-start.38 = (bf16[256,1024]{1,0:T(8,128)(2,1)S(1)}, bf16[256,1024]{1,0:T(8,128)(2,1)S(1)}, u32[]{:S(2)}, u32[]{:S(2)}) collective-permute-start(bf16[256,1024]{1,0:T(8,128)(2,1)S(1)} %fusion.12), channel_id=1, source_target_pairs={{0,2},{2,0},{4,6},{6,4},{8,10},{10,8},{12,14},{14,12},{16,18},{18,... | collective-permute-start | bytes 1572872 | tf_op jit(solution)/shard_map/ppermute | solution.py:256
  390.5 40.8 %collective-permute-start.41 = (bf16[256,1024]{1,0:T(8,128)(2,1)S(1)}, bf16[256,1024]{1,0:T(8,128)(2,1)S(1)}, u32[]{:S(2)}, u32[]{:S(2)}) collective-permute-start(bf16[256,1024]{1,0:T(8,128)(2,1)S(1)} %fusion.13), channel_id=1, source_target_pairs={{0,4},{2,6},{4,0},{6,2},{8,12},{10,14},{12,8},{14,10},{16,20},{18,... | collective-permute-start | bytes 1572872 | tf_op jit(solution)/shard_map/ppermute | solution.py:259
  431.3 47.6 %collective-permute-start.32 = (bf16[256,1024]{1,0:T(8,128)(2,1)S(1)}, bf16[256,1024]{1,0:T(8,128)(2,1)}, u32[]{:S(2)}, u32[]{:S(2)}) collective-permute-start(bf16[256,1024]{1,0:T(8,128)(2,1)S(1)} %fusion.9), channel_id=1, source_target_pairs={{0,4},{2,6},{4,0},{6,2},{8,12},{10,14},{12,8},{14,10},{16,20},{18,... | collective-permute-start | bytes 1572872 | tf_op jit(solution)/shard_map/ppermute | solution.py:259
  438.7 36.5 %collective-permute-start.29 = (f32[128,128]{1,0:T(8,128)S(1)}, f32[128,128]{1,0:T(8,128)S(1)}, u32[]{:S(2)}, u32[]{:S(2)}) collective-permute-start(f32[128,128]{1,0:T(8,128)S(1)} %get-tuple-element.54), channel_id=1, source_target_pairs={{0,16},{2,18},{4,20},{6,22},{8,24},{10,26},{12,28},{14,30},{16,0},... | collective-permute-start | bytes 196616 | tf_op jit(solution)/shard_map/ppermute | solution.py:262
  440.5 35.7 %collective-permute-start.30 = (f32[128,128]{1,0:T(8,128)S(1)}, f32[128,128]{1,0:T(8,128)S(1)}, u32[]{:S(2)}, u32[]{:S(2)}) collective-permute-start(f32[128,128]{1,0:T(8,128)S(1)} %get-tuple-element.53), channel_id=1, source_target_pairs={{0,24},{2,26},{4,28},{6,30},{8,0},{10,2},{12,4},{14,6},{16,8},{18,... | collective-permute-start | bytes 196616 | tf_op jit(solution)/shard_map/ppermute | solution.py:262
  442.9 65.3 %collective-permute-start.39 = (bf16[256,2048]{1,0:T(8,128)(2,1)}, bf16[256,2048]{1,0:T(8,128)(2,1)}, u32[]{:S(2)}, u32[]{:S(2)}) collective-permute-start(bf16[256,2048]{1,0:T(8,128)(2,1)} %pad_maximum_fusion), channel_id=1, source_target_pairs={{0,16},{2,18},{4,20},{6,22},{8,24},{10,26},{12,28},{14,30},{16,0},... | collective-permute-start | bytes 3145736 | tf_op jit(solution)/shard_map/ppermute | solution.py:262
  445.4 62.8 %collective-permute-start.44 = (bf16[256,2048]{1,0:T(8,128)(2,1)}, bf16[256,2048]{1,0:T(8,128)(2,1)}, u32[]{:S(2)}, u32[]{:S(2)}) collective-permute-start(bf16[256,2048]{1,0:T(8,128)(2,1)} %pad_maximum_fusion.1), channel_id=1, source_target_pairs={{0,8},{2,10},{4,12},{6,14},{8,16},{10,18},{12,20},{14,22},{16,24},... | collective-permute-start | bytes 3145736 | tf_op jit(solution)/shard_map/ppermute | solution.py:262
  475.2 41.7 %collective-permute-start.49 = (bf16[256,2048]{1,0:T(8,128)(2,1)}, bf16[256,2048]{1,0:T(8,128)(2,1)}, u32[]{:S(2)}, u32[]{:S(2)}) collective-permute-start(bf16[256,2048]{1,0:T(8,128)(2,1)} %pad_maximum_fusion.2), channel_id=1, source_target_pairs={{0,24},{2,26},{4,28},{6,30},{8,0},{10,2},{12,4},{14,6},{16,8},{18,... | collective-permute-start | bytes 3145736 | tf_op jit(solution)/shard_map/ppermute | solution.py:262
  (50 other events, 1007.3 us)
Sparse Core Ops, SparseCore 0:
  9.5 22.5 all-gather.1
